TPU v7x, 256 devices: a whole 4x4x8 slice. The times are simulated.
256 devices in a mesh: group: 8 (over y, core), owner: 32 (over x, z).
Axes of the slice: x: 4, y: 4, z: 8, core: 2. Of those that a mesh axis runs over, the one named last changes fastest.
Arguments:
- first_table: float32 [8, 16384, 400], P('group', 'owner'), may hold values from -1.5 to 1.5
- first_state: float32 [8, 16384], P('group', 'owner'), may hold values from 0.001 to 0.01
- second_table: float32 [8, 16384, 400], P('group', 'owner'), may hold values from -1.5 to 1.5
- second_state: float32 [8, 16384], P('group', 'owner'), may hold values from 0.001 to 0.01
- relation_diag: float32 [2304, 400], replicated, may hold values from 0.5 to 1.5
- relation_state: float32 [2304], replicated, may hold values from 0.001 to 0.01
- source_row: int32 [8, 32768], P('group', 'owner'), may hold values from 0 to 511
- target_owner: int32 [8, 32768, 1], P('group', 'owner'), may hold values from 0 to 31; in each aligned block of 1024 rows (0 to 1023, 1024 to 2047, ..., all dimensions but the last counted through in order) at most 80 rows name the same one
- target_row: int32 [8, 32768], P('group', 'owner'), may hold values from 0 to 511
- relation_id: int32 [8, 32768], P('group', 'owner'), may hold values from 0 to 2303
- negative_id: int32 [8, 2, 100], P('group'), may hold values from 0 to 16383
Outputs:
- first_new: float32 [8, 16384, 400], P('group', 'owner')
- first_state_new: float32 [8, 16384], P('group', 'owner')
- second_new: float32 [8, 16384, 400], P('group', 'owner')
- second_state_new: float32 [8, 16384], P('group', 'owner')
- relation_new: float32 [2304, 400], replicated
- relation_state_new: float32 [2304], replicated
Inputs may be any that keep to these rules, and one draw needn't show every extreme that they name: `target_owner`: among the edges of one device, at most 80 name the same owner, and some device reaches 80.
All inputs are finite; a program needn't handle non-finite values.
Results may differ from a plain program's by a relative error of at most 0.0034.
The roundings to bfloat16 on the way count: a program that leaves them out, or rounds other values in their place, can miss the bound.
Values may be sent and summed in bfloat16 or wider, within the bound.
A program may use at most 128 MiB of HBM per device.

v0:
```python
import jax
import jax.numpy as jnp
from jax import lax
from jax.sharding import PartitionSpec as P

learn_rate = 0.1


def adagrad_rows(table, state, grad):
    state_new = state + jnp.mean(grad * grad, axis=-1)
    return (table - learn_rate * grad / jnp.sqrt(state_new)[:, None], state_new)


def place_slots(owners, parts, capacity):
    onehot = (owners[:, None] == jnp.arange(parts, dtype=jnp.int32)[None, :]).astype(jnp.int32)
    before = jnp.cumsum(onehot, axis=0) - onehot
    slots = jnp.sum(before * onehot, axis=1)
    return owners * capacity + slots


def bucket_grads(
    src_table, dst_table, relation_diag, src_row, dst_owner, dst_row, kinds, negatives
):
    parts = lax.axis_size("owner")
    owner_index = lax.axis_index("owner")
    edge_count = dst_owner.shape[0]
    width = src_table.shape[1]
    local_rows = src_table.shape[0]
    capacity = 5 * edge_count // (2 * parts)
    src_copy = src_table.astype(jnp.bfloat16)
    dst_copy = dst_table.astype(jnp.bfloat16)
    dst_place = place_slots(dst_owner, parts, capacity)
    empty_ids = jnp.zeros((parts * capacity,), jnp.int32)
    dst_request = empty_ids.at[dst_place].set(dst_row).reshape(parts, capacity)
    asked_dst = lax.all_to_all(dst_request, "owner", split_axis=0, concat_axis=0, tiled=True)
    served_dst = dst_copy[asked_dst]
    back_dst = lax.all_to_all(served_dst, "owner", split_axis=0, concat_axis=0, tiled=True)
    src_rows = src_copy[src_row]
    dst_rows = back_dst.reshape(parts * capacity, width)[dst_place]
    blocks = negatives.shape[0]
    neg_count = negatives.shape[1]
    neg_owner = negatives // local_rows
    neg_local = negatives - neg_owner * local_rows
    neg_mine = neg_owner == owner_index
    offered = jnp.where(neg_mine[..., None], dst_copy[neg_local], jnp.zeros((), jnp.bfloat16))
    neg_rows = lax.psum(offered, "owner").astype(jnp.float32).astype(jnp.bfloat16)
    rel_rows = relation_diag[kinds]
    queries = (src_rows.astype(jnp.float32) * rel_rows).astype(jnp.bfloat16)
    block_size = edge_count // blocks
    query_blocks = queries.reshape(blocks, block_size, width)
    target_blocks = dst_rows.reshape(blocks, block_size, width)
    batch = jnp.einsum(
        "kcd,kjd->kcj", query_blocks, target_blocks, preferred_element_type=jnp.float32
    )
    sampled = jnp.einsum("kcd,knd->kcn", query_blocks, neg_rows, preferred_element_type=jnp.float32)
    scale = 1.0 / (block_size - 1 + neg_count)
    diagonal = jnp.eye(block_size, dtype=bool)[None]
    d_batch = jnp.where(diagonal, -jax.nn.sigmoid(-batch), scale * jax.nn.sigmoid(batch)).astype(
        jnp.bfloat16
    )
    d_sampled = (scale * jax.nn.sigmoid(sampled)).astype(jnp.bfloat16)
    d_query = jnp.einsum("kcj,kjd->kcd", d_batch, target_blocks, preferred_element_type=jnp.float32)
    d_query = d_query + jnp.einsum(
        "kcn,knd->kcd", d_sampled, neg_rows, preferred_element_type=jnp.float32
    )
    d_target = (
        jnp.einsum("kcj,kcd->kjd", d_batch, query_blocks, preferred_element_type=jnp.float32)
        .astype(jnp.bfloat16)
        .reshape(edge_count, width)
    )
    d_negative = jnp.einsum(
        "kcn,kcd->knd", d_sampled, query_blocks, preferred_element_type=jnp.float32
    )
    d_query = d_query.reshape(edge_count, width)
    d_source = (d_query * rel_rows).astype(jnp.bfloat16)
    d_relation = jax.ops.segment_sum(
        d_query * src_rows.astype(jnp.float32), kinds, num_segments=relation_diag.shape[0]
    )
    src_grad = jax.ops.segment_sum(d_source.astype(jnp.float32), src_row, num_segments=local_rows)
    empty_rows = jnp.zeros((parts * capacity, width), jnp.bfloat16)
    send_dst = empty_rows.at[dst_place].set(d_target).reshape(parts, capacity, width)
    got_dst = lax.all_to_all(send_dst, "owner", split_axis=0, concat_axis=0, tiled=True)
    dst_grad = jax.ops.segment_sum(
        got_dst.reshape(parts * capacity, width).astype(jnp.float32),
        asked_dst.reshape(-1),
        num_segments=local_rows,
    )
    neg_total = lax.psum(d_negative.astype(jnp.bfloat16), "owner").astype(jnp.float32)
    neg_kept = jnp.where(neg_mine[..., None], neg_total, 0.0).reshape(blocks * neg_count, width)
    dst_grad = dst_grad + jax.ops.segment_sum(
        neg_kept, neg_local.reshape(-1), num_segments=local_rows
    )
    return (src_grad, dst_grad, d_relation)


def on_device(
    first_table,
    first_state,
    second_table,
    second_state,
    relation_diag,
    relation_state,
    source_row,
    target_owner,
    target_row,
    relation_id,
    negative_id,
):
    src_grad, dst_grad, d_relation = bucket_grads(
        first_table[0],
        second_table[0],
        relation_diag,
        source_row[0],
        target_owner[0, :, 0],
        target_row[0],
        relation_id[0],
        negative_id[0],
    )
    first_new, first_state_new = adagrad_rows(first_table[0], first_state[0], src_grad)
    second_new, second_state_new = adagrad_rows(second_table[0], second_state[0], dst_grad)
    share = lax.psum_scatter(d_relation, ("group", "owner"), scatter_dimension=0, tiled=True)
    share_rows = share.shape[0]
    start = lax.axis_index(("group", "owner")) * share_rows
    diag_part = lax.dynamic_slice_in_dim(relation_diag, start, share_rows, 0)
    state_part = lax.dynamic_slice_in_dim(relation_state, start, share_rows, 0)
    diag_part, state_part = adagrad_rows(diag_part, state_part, share)
    relation_new, relation_state_new = (
        lax.all_gather(diag_part, ("group", "owner"), axis=0, tiled=True),
        lax.all_gather(state_part, ("group", "owner"), axis=0, tiled=True),
    )
    return (
        first_new[None],
        first_state_new[None],
        second_new[None],
        second_state_new[None],
        relation_new,
        relation_state_new,
    )


def solution(mesh):
    in_specs = (
        P("group", "owner", None),
        P("group", "owner"),
        P("group", "owner", None),
        P("group", "owner"),
        P(),
        P(),
        P("group", "owner"),
        P("group", "owner", None),
        P("group", "owner"),
        P("group", "owner"),
        P("group", None, None),
    )
    out_specs = (
        P("group", "owner", None),
        P("group", "owner"),
        P("group", "owner", None),
        P("group", "owner"),
        P(),
        P(),
    )
    return jax.shard_map(
        on_device, mesh=mesh, in_specs=in_specs, out_specs=out_specs, check_vma=False
    )
```

profile of v0, /device:TPU:1, one launch (start us, length us, event | category | flops | bytes accessed | tf_op | source)
XLA Modules:
  0.0 801.6 jit_solution(1610017823931083903)
XLA Ops:
  7.9 9.0 %reduce-window.6 = s32[32,8,128]{2,1,0:T(8,128)S(1)} reduce-window(s32[32,8,128]{2,1,0:T(8,128)S(1)} %fusion.24, s32[]{:T(128)} %constant.21.clone.1), window={size=1x1x128 pad=0_0x0_0x127_0}, to_apply=%region_0.0 | reduce-window | flops 4161536 | bytes 262148 | tf_op jit(solution)/shard_map/reduce-window
  18.8 4.5 scatter_custom_fusion
  24.0 11.9 %all-to-all-start = ((s32[32,1,80]{2,1,0:T(1,128)}), s32[32,1,80]{2,1,0:T(1,128)S(1)}, u32[]{:S(2)}, u32[]{:S(2)}) async-start(s32[32,1,80]{2,1,0:T(1,128)} %all_to_all.14), calls=%async_computation | async-start | bytes 32768 | tf_op jit(solution)/shard_map/all_to_all | solution.py:35
  37.4 7.0 all-to-all-done
  44.5 8.2 %gather_fusion.2 = bf16[2560,400]{1,0:T(8,128)(2,1)} fusion(bf16[512,400]{1,0:T(8,128)(2,1)S(1)} %bitcast_convert_fusion, s32[3072]{0:T(1024)S(1)} %pad_clamp_fusion), kind=kCustom, calls=%fused_computation.2 | custom fusion | bytes 4106240 | tf_op jit(solution)/shard_map/gather | solution.py:36
  52.7 4.2 all-to-all-start.1
  61.8 5.6 copy.73
  68.7 5.1 gather_fusion
  73.8 7.6 gather_fusion.1
  81.4 3.2 fusion.4
  84.7 122.9 %all-reduce.6.cloned.1.call-done = bf16[2,100,400]{1,2,0:T(8,128)(2,1)} async-done(((bf16[2,100,400]{1,2,0:T(8,128)(2,1)}), bf16[2,100,400]{1,2,0:T(8,128)(2,1)}) %all-reduce.6.cloned.1.call-update) | async-done | bytes 160016 | tf_op jit(solution)/shard_map/psum | solution.py:46
  209.4 5.1 gather_fusion.3
  214.5 3.2 select_convert_fusion
  222.3 9.2 %scatter_custom_fusion.5 = f32[2304,400]{1,0:T(8,128)} fusion(s32[1024]{0:T(1024)S(1)} %bitcast.135, f32[]{:T(128)} %constant.19.clone.1, f32[1024,400]{1,0:T(8,128)S(1)} %bitcast.111, bf16[1024,400]{1,0:T(8,128)(2,1)S(1)} %copy-done.2), kind=kCustom, calls=%fused_computation.15 | custom fusion | flops 1228800 | bytes 6832132 | tf_op jit(solution)/shard_map/scatter-add | solution.py:76
  234.1 269.1 %all-reduce.10.cloned.1.call-done = f32[2304,400]{1,0:T(8,128)} async-done(((f32[2304,400]{1,0:T(8,128)}), f32[2304,400]{1,0:T(8,128)}) %all-reduce.10.cloned.1.call-update) | async-done | bytes 3686416
  507.9 7.0 scatter_custom_fusion.2
  514.8 9.8 %all-to-all-start.2 = ((bf16[32,80,400]{2,1,0:T(8,128)(2,1)}), bf16[32,80,400]{2,1,0:T(8,128)(2,1)}, u32[]{:S(2)}, u32[]{:S(2)}) async-start(bf16[32,80,400]{2,1,0:T(8,128)(2,1)} %bitcast.26), calls=%async_computation.2 | async-start | bytes 5242880 | tf_op jit(solution)/shard_map/all_to_all | solution.py:82
  527.2 130.1 %all-reduce.8.cloned.1.call-done = bf16[2,100,400]{1,2,0:T(8,128)(2,1)} async-done(((bf16[2,100,400]{1,2,0:T(8,128)(2,1)}), bf16[2,100,400]{1,2,0:T(8,128)(2,1)}) %all-reduce.8.cloned.1.call-update) | async-done | bytes 160016 | tf_op jit(solution)/shard_map/psum | solution.py:88
  663.7 7.5 scatter_custom_fusion.1
  675.6 78.5 %all-reduce = f32[2304]{0:T(1024)} all-reduce(f32[2304]{0:T(1024)S(1)} %copy-done.12), channel_id=1, replica_groups=mesh['group'=8,'owner'=32] {'group','owner'}, use_global_device_ids=true, to_apply=%add | all-reduce | flops 2304 | bytes 18432
  754.1 18.2 %scatter_custom_fusion.3 = f32[512,400]{1,0:T(8,128)S(1)} fusion(s32[2560]{0:T(1024)} %reshape.474, bf16[2560,400]{1,0:T(8,128)(2,1)} %bitcast.35, f32[]{:T(128)} %constant.19.clone.1), kind=kCustom, calls=%fused_computation.11 | custom fusion | flops 2048000 | bytes 3441152 | tf_op jit(solution)/shard_map/scatter-add | solution.py:83
  776.7 5.6 all-gather.3.cloned.1.call-done
  782.3 7.2 reshape.504
  789.5 5.6 copy.93
  (108 shorter events, 42.2 us)
Async XLA Ops:
  24.0 20.4 %all-to-all-start = ((s32[32,1,80]{2,1,0:T(1,128)}), s32[32,1,80]{2,1,0:T(1,128)S(1)}, u32[]{:S(2)}, u32[]{:S(2)}) async-start(s32[32,1,80]{2,1,0:T(1,128)} %all_to_all.14), calls=%async_computation | async-start | bytes 32768 | tf_op jit(solution)/shard_map/all_to_all | solution.py:35
  37.3 15.4 %copy-start.3 = (f32[1,512,400]{2,1,0:T(8,128)}, f32[1,512,400]{2,1,0:T(8,128)S(1)}, u32[]{:S(2)}) copy-start(f32[1,512,400]{2,1,0:T(8,128)S(1)} %copy.74) | copy-start | bytes 2457604
  52.7 4.3 copy-start.13
  52.7 156.7 %all-to-all-start.1 = ((bf16[32,80,400]{2,1,0:T(8,128)(2,1)}), bf16[32,80,400]{2,1,0:T(8,128)(2,1)S(1)}, u32[]{:S(2)}, u32[]{:S(2)}) async-start(bf16[32,80,400]{2,1,0:T(8,128)(2,1)} %bitcast.112), calls=%async_computation.1 | async-start | bytes 5242880 | tf_op jit(solution)/shard_map/all_to_all | solution.py:37
  56.9 150.7 %all-reduce.6.cloned.1.call-start = ((), (), s32[]{:S(2)}) async-start(), calls=%async_computation.3 | async-start | bytes 409600 | tf_op jit(solution)/shard_map/psum | solution.py:46
  59.1 444.0 %all-reduce.10.cloned.1.call-start = ((), (), s32[]{:S(2)}) async-start(), calls=%async_computation.6 | async-start | bytes 9437184
  61.8 5.6 copy-start.17
  68.7 5.1 copy-start.16
  214.5 3.2 copy-start.7
  217.7 1.2 copy-start.10
  220.4 2.0 copy-start.2
  222.3 9.3 %copy-start.1 = (f32[2,512,400]{2,1,0:T(8,128)}, f32[2,512,400]{2,1,0:T(8,128)S(1)}, u32[]{:S(2)}) copy-start(f32[2,512,400]{2,1,0:T(8,128)S(1)} %copy.101) | copy-start | bytes 4915204
  231.6 1.2 copy-start.6
  231.6 275.1 %copy-start.9 = (bf16[2,512,512]{2,1,0:T(8,128)(2,1)S(1)}, bf16[2,512,512]{2,1,0:T(8,128)(2,1)}, u32[]{:S(2)}) copy-start(bf16[2,512,512]{2,1,0:T(8,128)(2,1)} %copy-done.8) | copy-start | bytes 3145732
  231.6 425.7 %all-reduce.8.cloned.1.call-start = ((), (), s32[]{:S(2)}) async-start(), calls=%async_computation.4 | async-start | bytes 409600 | tf_op jit(solution)/shard_map/psum | solution.py:88
  234.0 548.3 %all-gather.3.cloned.1.call-start = ((), (), s32[]{:S(2)}) async-start(), calls=%async_computation.5 | async-start | bytes 8421376 | tf_op jit(solution)/shard_map/all_gather | solution.py:128
  505.1 1.5 copy-start.11
  514.8 239.2 %all-to-all-start.2 = ((bf16[32,80,400]{2,1,0:T(8,128)(2,1)}), bf16[32,80,400]{2,1,0:T(8,128)(2,1)}, u32[]{:S(2)}, u32[]{:S(2)}) async-start(bf16[32,80,400]{2,1,0:T(8,128)(2,1)} %bitcast.26), calls=%async_computation.2 | async-start | bytes 5242880 | tf_op jit(solution)/shard_map/all_to_all | solution.py:82
  524.6 136.1 %copy-start = (f32[1024,400]{1,0:T(8,128)S(1)}, f32[1024,400]{1,0:T(8,128)}, u32[]{:S(2)}) copy-start(f32[1024,400]{1,0:T(8,128)} %gather_fusion.1) | copy-start | bytes 4915204
  663.7 7.7 copy-start.14
  663.7 7.7 copy-start.5
  671.4 4.2 copy-start.12
  754.1 18.4 %copy-start.15 = (f32[1,512]{1,0:T(1,128)S(1)}, f32[1,512]{1,0:T(1,128)}, u32[]{:S(2)}) copy-start(f32[1,512]{1,0:T(1,128)} %param.14) | copy-start | bytes 6148
  754.1 18.5 %copy-start.4 = (f32[1,512,400]{2,1,0:T(8,128)S(1)}, f32[1,512,400]{2,1,0:T(8,128)}, u32[]{:S(2)}) copy-start(f32[1,512,400]{2,1,0:T(8,128)} %copy-done.3) | copy-start | bytes 2457604
  (1 other events, 1.0 us)
Sparse Core Ops, SparseCore 0:
  61.8 145.8 all-reduce.5
  231.7 271.3 all-reduce.9
  507.5 149.7 all-reduce.7
  661.5 120.7 all-gather.2
where the time goes:
time: 803 us; the launch traced here: 802 us
  waiting for transfers between devices  535 us (67%)
  blocking collectives  78.5 us (10%)
  local copies, waits for them, and re-layouts  72.7 us (9%)
  other arithmetic  66.4 us (8%)
  starting transfers between devices  26.2 us (3%)
  between operations  14.2 us (2%)
  matrix products  8.88 us (1%)
    unnamed x5, waiting for transfers between devices  269 us
    psum x1, waiting for transfers between devices, bucket_grads(): lax.psum(d_negative.astype(jnp.bfloat16), 'owner').astype(jnp.float32)  130 us
    psum x1, waiting for transfers between devices, bucket_grads(): lax.psum(offered, 'owner').astype(jnp.float32).astype(jnp.bfloat16)  123 us
    unnamed x1, blocking collectives  78.5 us
    unnamed x44, local copies, waits for them, and re-layouts  28.9 us
    scatter-add x1, other arithmetic, bucket_grads(): jax.ops.segment_sum(got_dst.reshape(parts * capacity, width).astype(jnp.f...  18.2 us
  transfers between devices with their start and end apart: 7, of which 5 were waited for; matrix products, arithmetic and copies ran while one was open for 11% of the time, Pallas kernels for 0%

commit v1 on v0

v1 whole, which is shorter than its diff:
```python
import jax
import jax.numpy as jnp
from jax import lax
from jax.experimental import pallas as pl
from jax.experimental.pallas import tpu as pltpu
from jax.sharding import PartitionSpec as P

MESH = pl.DeviceIdType.MESH
F32 = jnp.float32
BF16 = jnp.bfloat16
LEARN = 0.1

D = 400
R = 512
E = 1024
BLOCK = 512
NEG = 100
NL = 128
K = 2304
NX, NY, NZ = 4, 4, 8
SLOTS = 256

GROUPS = ((0, 1, 7), (2, 6), (3, 5, 4))
CUTS = ((0, 96), (96, 112), (208, 96), (304, 96))
UP = (0, 7, 6, 5, 4)
DOWN = (0, 1, 2, 3, 4)
HALF = 208

H_CORE, H_Y, H_X, H_Z = 4096, 1024, 256, 32

NN = (((1,), (0,)), ((), ()))
NT = (((1,), (1,)), ((), ()))
TN = (((0,), (0,)), ((), ()))


def dot(a, b, dims):
    return lax.dot_general(a, b, dims, preferred_element_type=F32)


def onehot(vec, base, n):
    rows = lax.broadcasted_iota(jnp.int32, (n, vec.shape[1]), 0)
    return jnp.where(rows == vec - base, 1.0, 0.0).astype(BF16)


def adagrad(table, state, grad):
    state_new = state + jnp.sum(grad * grad, axis=0, keepdims=True) * (1.0 / D)
    return table - LEARN * grad * (1.0 / jnp.sqrt(state_new)), state_new


def step_kernel(
    first_ref, fstate_ref, second_ref, sstate_ref, diag_ref,
    srow_ref, towner_ref, trow_ref, kind_ref, neg_ref,
    first_new, fstate_new, second_new, sstate_new, rel_out,
    tabs, req, asked, serve, back, negpart, place_ref,
    splits, relrow, srcrow, query, dst, summand, dsource, dtarget, dneg, dnegpart,
    csend, crecv, up_send, up_recv, down_send, down_recv,
    relbuf, core_recv, y_recv, x_recv, z_recv, red_y, red_x,
    ag_s, ag_r, rq_s, rq_r, sv_s, sv_r, ng_s, ng_r, cs_s, cs_r, dn_s, dn_r, rs_s, rs_r,
    co_s, co_r, ry_s, ry_r, rx_s, rx_r, rz_s, rz_r,
):
    g = lax.axis_index("group")
    o = lax.axis_index("owner")
    x, z = o // NZ, o % NZ
    y, c = g // 2, g % 2

    def dev_x(k):
        return (g, lax.rem(x + k, NX) * NZ + z)

    def dev_z(k):
        return (g, x * NZ + lax.rem(z + k, NZ))

    def dev_y(k):
        return (lax.rem(y + k, NY) * 2 + c, o)

    dev_c = (y * 2 + 1 - c, o)

    barrier = pltpu.get_barrier_semaphore()
    for peer in [dev_x(k) for k in range(1, NX)] + [dev_z(k) for k in range(1, NZ)] + [
        dev_y(k) for k in range(1, NY)
    ] + [dev_c]:
        pl.semaphore_signal(barrier, inc=1, device_id=peer, device_id_type=MESH)
    tabs[0] = second_ref[...].astype(BF16)
    pl.semaphore_wait(barrier, NX + NZ + NY - 3 + 1)

    def remote(src, dst_, ss, rs, dev):
        return pltpu.make_async_remote_copy(
            src_ref=src, dst_ref=dst_, send_sem=ss, recv_sem=rs, device_id=dev, device_id_type=MESH
        )

    def gather_copy(way, step, q):
        path = UP if way == 0 else DOWN
        rows = pl.ds(*CUTS[q])
        return remote(
            tabs.at[path[step], rows], tabs.at[path[step + 1], rows],
            ag_s.at[way, step, q], ag_r.at[way, step, q], dev_z(1 if way == 0 else NZ - 1),
        )

    def gather_cuts(way, step):
        return range(4) if step < 3 else ((0, 1) if way == 0 else (2, 3))

    for q in range(4):
        for way in (0, 1):
            gather_copy(way, 0, q).start()

    def forward(step):
        for q in range(4):
            for way in (0, 1):
                if q in gather_cuts(way, step):
                    gather_copy(way, step, q).wait_recv()
                    if step < 3 and q in gather_cuts(way, step + 1):
                        gather_copy(way, step + 1, q).start()

    towner, trow = towner_ref[...], trow_ref[...]
    far = lax.rem(towner % NZ - z + NZ, NZ)
    side = lax.rem(towner // NZ - x + NX, NX)
    group = jnp.zeros_like(far)
    local = jnp.zeros_like(far)
    for gi, members in enumerate(GROUPS):
        for li, offset in enumerate(members):
            group = jnp.where(far == offset, gi, group)
            local = jnp.where(far == offset, li, local)
    kind_of = side * 8 + group
    mine = jnp.where(lax.broadcasted_iota(jnp.int32, (32, E), 0) == kind_of, 1.0, 0.0)
    before_mask = jnp.where(
        lax.broadcasted_iota(jnp.int32, (E, E), 0) < lax.broadcasted_iota(jnp.int32, (E, E), 1), 1.0, 0.0
    ).astype(BF16)
    before = dot(mine.astype(BF16), before_mask, NN)
    slot = jnp.sum(mine * before, axis=0, keepdims=True).astype(jnp.int32)
    place_ref[...] = kind_of * SLOTS + slot
    value = local * R + trow + 1
    high = (value // 16).astype(F32)
    low = (value % 16).astype(F32)
    sends = jnp.concatenate([mine * high, mine * low], axis=0).astype(BF16)
    found = dot(sends, onehot(slot, 0, SLOTS), NT)
    wanted = (found[0:32] * 16.0 + found[32:64]).astype(jnp.int32) - 1
    asked[0] = wanted[0:8]
    for k in range(1, NX):
        req[k] = wanted[8 * k : 8 * k + 8]

    def req_copy(k):
        return remote(req.at[k], asked.at[NX - k], rq_s.at[k], rq_r.at[NX - k], dev_x(k))

    for k in range(1, NX):
        req_copy(k).start()

    first_copy = first_ref[...].astype(BF16)
    for b in range(2):
        lanes = slice(b * BLOCK, (b + 1) * BLOCK)
        srcrow[:, lanes] = dot(first_copy, onehot(srow_ref[:, lanes], 0, R), NN).astype(BF16)
    diag = diag_ref[...]
    high_part = diag.astype(BF16)
    rest = diag - high_part.astype(F32)
    splits[0] = high_part
    splits[1] = rest.astype(BF16)
    splits[2] = (rest - splits[1].astype(F32)).astype(BF16)

    for k in range(1, NX):
        remote(req.at[k], asked.at[k], rq_s.at[k], rq_r.at[k], dev_x(k)).wait_recv()

    def serve_copy(j, gi):
        return remote(
            serve.at[j, gi], back.at[NX - j, gi], sv_s.at[j, gi], sv_r.at[NX - j, gi], dev_x(j)
        )

    def serve_rows(j, gi):
        want = asked[j][gi : gi + 1, :]
        total = None
        for li, offset in enumerate(GROUPS[gi]):
            part = dot(tabs[offset], onehot(want, li * R, R), NN)
            total = part if total is None else total + part
        return total.astype(BF16)

    def serve_group(gi):
        def body(j, carry):
            serve[j, gi] = serve_rows(j, gi)
            serve_copy(j, gi).start()
            return carry

        lax.fori_loop(1, NX, body, 0)
        back[0, gi] = serve_rows(0, gi)

    def relation_rows(n):
        def body(i, carry):
            lanes = pl.ds(pl.multiple_of(i * 128, 128), 128)
            pick = onehot(kind_ref[:, lanes], 0, K)
            relrow[:, lanes] = (
                dot(splits[0], pick, NN) + dot(splits[1], pick, NN) + dot(splits[2], pick, NN)
            )
            return carry

        lax.fori_loop(n * 4, n * 4 + 4, body, 0)

    def wait_back(gi):
        for k in range(1, NX):
            remote(serve.at[k, gi], back.at[k, gi], sv_s.at[k, gi], sv_r.at[k, gi], dev_x(k)).wait_recv()

    def collect(gi, first):
        for b in range(2):
            lanes = slice(b * BLOCK, (b + 1) * BLOCK)

            def body(k, total):
                pick = onehot(place_ref[:, lanes], (k * 8 + gi) * SLOTS, SLOTS)
                return total + dot(back[k, gi], pick, NN)

            start = jnp.zeros((D, BLOCK), F32) if first else dst[:, lanes].astype(F32)
            dst[:, lanes] = lax.fori_loop(0, NX, body, start).astype(BF16)

    forward(0)
    serve_group(0)
    relation_rows(0)
    forward(1)
    serve_group(1)
    relation_rows(1)
    query[...] = (srcrow[...].astype(F32) * relrow[...]).astype(BF16)
    forward(2)
    forward(3)

    negs = neg_ref[...] - x * (NZ * R)
    line = jnp.zeros((D, 2 * NL), F32)
    for offset in range(NZ):
        line = line + dot(tabs[offset], onehot(negs, lax.rem(z + offset, NZ) * R, R), NN)
    negpart[0] = line.astype(BF16)

    def neg_copy(k):
        return remote(negpart.at[0], negpart.at[NX - k], ng_s.at[k], ng_r.at[NX - k], dev_x(k))

    serve_group(2)
    for k in range(1, NX):
        neg_copy(k).start()
    wait_back(0)
    collect(0, True)
    wait_back(1)
    collect(1, False)
    wait_back(2)
    collect(2, False)
    for k in range(1, NX):
        remote(negpart.at[0], negpart.at[k], ng_s.at[k], ng_r.at[k], dev_x(k)).wait_recv()
    negrow = (
        negpart[0].astype(F32) + negpart[1].astype(F32) + negpart[2].astype(F32) + negpart[3].astype(F32)
    ).astype(BF16)

    scale = 1.0 / (BLOCK - 1 + NEG)
    diagonal = lax.broadcasted_iota(jnp.int32, (BLOCK, BLOCK), 0) == lax.broadcasted_iota(
        jnp.int32, (BLOCK, BLOCK), 1
    )
    for b in range(2):
        lanes = slice(b * BLOCK, (b + 1) * BLOCK)
        nl = slice(b * NL, (b + 1) * NL)
        q, t, n = query[:, lanes], dst[:, lanes], negrow[:, nl]
        batch = dot(q, t, TN)
        sampled = dot(q, n, TN)
        d_batch = (
            jax.nn.sigmoid(jnp.where(diagonal, -batch, batch)) * jnp.where(diagonal, -1.0, scale)
        ).astype(BF16)
        d_sampled = (scale * jax.nn.sigmoid(sampled)).astype(BF16)
        d_query = dot(t, d_batch, NT) + dot(n, d_sampled, NT)
        dsource[:, lanes] = (d_query * relrow[:, lanes]).astype(BF16)
        summand[:, lanes] = (d_query * srcrow[:, lanes].astype(F32)).astype(BF16)
        dtarget[:, lanes] = dot(q, d_batch, NN).astype(BF16)
        dneg[:, nl] = dot(q, d_sampled, NN).astype(BF16)

    for half in range(2):
        relbuf[pl.ds(half * H_CORE + 3600, H_CORE - 3600)] = jnp.zeros((H_CORE - 3600, 128), BF16)

    def relation_part(i, carry):
        pick = onehot(kind_ref[...], i * 128, 128)
        start = pl.multiple_of((i // 9) * H_CORE + (i % 9) * D, 16)
        relbuf[pl.ds(start, D)] = dot(summand[...], pick, NT).astype(BF16)
        return carry

    def core_copy():
        other = pl.ds(pl.multiple_of((1 - c) * H_CORE, H_CORE), H_CORE)
        return remote(relbuf.at[other], core_recv, co_s.at[0], co_r.at[0], dev_c)

    lax.fori_loop(0, 18, relation_part, 0)
    core_copy().start()

    def c_copy(j, gi):
        return remote(
            csend.at[j, gi], crecv.at[NX - j, gi], cs_s.at[j, gi], cs_r.at[NX - j, gi], dev_x(j)
        )

    def spread(j, gi):
        pick = onehot(place_ref[...], (j * 8 + gi) * SLOTS, SLOTS)
        return dot(dtarget[...], pick, NT).astype(BF16)

    def send_group(gi):
        def body(j, carry):
            csend[j, gi] = spread(j, gi)
            c_copy(j, gi).start()
            return carry

        lax.fori_loop(1, NX, body, 0)
        crecv[0, gi] = spread(0, gi)

    def dneg_copy(k):
        return remote(dneg, dnegpart.at[NX - k], dn_s.at[k], dn_r.at[NX - k], dev_x(k))

    for k in range(1, NX):
        dneg_copy(k).start()
    send_group(2)

    core_copy().wait_recv()
    own = pl.ds(pl.multiple_of(c * H_CORE, H_CORE), H_CORE)
    relbuf[own] = (relbuf[own].astype(F32) + core_recv[...].astype(F32)).astype(BF16)

    def rel_rows(cc, yy, xx, zz, n):
        return pl.ds(pl.multiple_of(cc * H_CORE + yy * H_Y + xx * H_X + zz * H_Z, 32), n)

    def ry_copy(k):
        rows = rel_rows(c, lax.rem(y + k, NY), 0, 0, H_Y)
        return remote(relbuf.at[rows], y_recv.at[NY - k], ry_s.at[0, k], ry_r.at[0, NY - k], dev_y(k))

    for k in range(1, NY):
        ry_copy(k).start()

    send_group(1)
    send_group(0)

    pick_src = onehot(srow_ref[...], 0, R)
    src_grad = dot(dsource[...], pick_src, NT)
    new_table, new_state = adagrad(first_ref[...], fstate_ref[...], src_grad)
    first_new[...] = new_table
    fstate_new[...] = new_state

    for k in range(1, NX):
        remote(dneg, dnegpart.at[k], dn_s.at[k], dn_r.at[k], dev_x(k)).wait_recv()
    neg_sum = dneg[...].astype(F32)
    for k in range(1, NX):
        neg_sum = neg_sum + dnegpart[k].astype(F32)
    dnegpart[0] = neg_sum.astype(BF16)

    def wait_c(gi):
        for k in range(1, NX):
            remote(csend.at[k, gi], crecv.at[k, gi], cs_s.at[k, gi], cs_r.at[k, gi], dev_x(k)).wait_recv()

    def line_sum(gi, li):
        offset = GROUPS[gi][li]
        total = dot(dnegpart[0], onehot(negs, lax.rem(z + offset, NZ) * R, R), NT)
        for k in range(NX):
            total = total + dot(crecv[k, gi], onehot(asked[k][gi : gi + 1, :], li * R, R), NT)
        return total

    def ring_copy(way, s, q):
        send, recv = (up_send, up_recv) if way == 0 else (down_send, down_recv)
        rows = pl.ds(*CUTS[q])
        return remote(
            send.at[s, rows], recv.at[s, rows], rs_s.at[way, s, q], rs_r.at[way, s, q],
            dev_z(1 if way == 0 else NZ - 1),
        )

    def ring_cuts(way, s):
        return range(4) if s > 0 else ((0, 1) if way == 0 else (2, 3))

    def ring_step(way, s, total):
        send, recv = (up_send, up_recv) if way == 0 else (down_send, down_recv)
        for q in range(4):
            at, size = CUTS[q]
            rows = slice(at, at + size)
            part = total[rows]
            if s > 0 and q in ring_cuts(way, s - 1):
                ring_copy(way, s - 1, q).wait_recv()
                part = part + recv[s - 1, rows].astype(F32)
            if q in ring_cuts(way, s):
                send[s, rows] = part.astype(BF16)
                ring_copy(way, s, q).start()

    wait_c(2)
    total = line_sum(2, 2)
    ring_step(0, 0, total)
    ring_step(1, 0, total)
    ring_step(0, 1, line_sum(2, 0))
    ring_step(1, 1, line_sum(2, 1))

    def wait_y():
        for k in range(1, NY):
            remote(y_recv.at[k], y_recv.at[k], ry_s.at[0, k], ry_r.at[0, k], dev_y(k)).wait_recv()

    wait_y()
    total = relbuf[rel_rows(c, y, 0, 0, H_Y)].astype(F32)
    for k in range(1, NY):
        total = total + y_recv[k].astype(F32)
    red_y[...] = total.astype(BF16)

    def rx_copy(k):
        rows = pl.ds(pl.multiple_of(lax.rem(x + k, NX) * H_X, H_X), H_X)
        return remote(red_y.at[rows], x_recv.at[NX - k], rx_s.at[0, k], rx_r.at[0, NX - k], dev_x(k))

    for k in range(1, NX):
        rx_copy(k).start()

    wait_c(1)
    ring_step(0, 2, line_sum(1, 0))
    ring_step(1, 2, line_sum(1, 1))

    for k in range(1, NX):
        remote(x_recv.at[k], x_recv.at[k], rx_s.at[0, k], rx_r.at[0, k], dev_x(k)).wait_recv()
    total = red_y[pl.ds(pl.multiple_of(x * H_X, H_X), H_X)].astype(F32)
    for k in range(1, NX):
        total = total + x_recv[k].astype(F32)
    red_x[...] = total.astype(BF16)

    def rz_copy(k):
        rows = pl.ds(pl.multiple_of(lax.rem(z + k, NZ) * H_Z, H_Z), H_Z)
        return remote(red_x.at[rows], z_recv.at[NZ - k], rz_s.at[0, k], rz_r.at[0, NZ - k], dev_z(k))

    for k in range(1, NZ):
        rz_copy(k).start()

    wait_c(0)
    near = line_sum(0, 1)
    for k in range(1, NZ):
        remote(z_recv.at[k], z_recv.at[k], rz_s.at[0, k], rz_r.at[0, k], dev_z(k)).wait_recv()
    total = red_x[pl.ds(pl.multiple_of(z * H_Z, H_Z), H_Z)].astype(F32)
    for k in range(1, NZ):
        total = total + z_recv[k].astype(F32)
    mine_rows = rel_rows(c, y, x, z, H_Z)
    rel_out[mine_rows] = total.astype(BF16)

    def back_copy(rows, ss, rs, dev):
        return remote(rel_out.at[rows], rel_out.at[rows], ss, rs, dev)

    for k in range(1, NZ):
        back_copy(mine_rows, rz_s.at[1, k], rz_r.at[1, NZ - k], dev_z(k)).start()

    ring_step(0, 3, near)
    ring_step(1, 3, line_sum(0, 2))

    for k in range(1, NZ):
        rows = rel_rows(c, y, x, lax.rem(z + k, NZ), H_Z)
        back_copy(rows, rz_s.at[1, k], rz_r.at[1, k], dev_z(k)).wait_recv()
    x_rows = rel_rows(c, y, x, 0, H_X)
    for k in range(1, NX):
        back_copy(x_rows, rx_s.at[1, k], rx_r.at[1, NX - k], dev_x(k)).start()
    total = line_sum(0, 0)
    for k in range(1, NX):
        rows = rel_rows(c, y, lax.rem(x + k, NX), 0, H_X)
        back_copy(rows, rx_s.at[1, k], rx_r.at[1, k], dev_x(k)).wait_recv()
    y_rows = rel_rows(c, y, 0, 0, H_Y)
    for k in range(1, NY):
        back_copy(y_rows, ry_s.at[1, k], ry_r.at[1, NY - k], dev_y(k)).start()

    for q in range(4):
        for way in (0, 1):
            ring_copy(way, 3, q).wait_recv()
    total = total + up_recv[3].astype(F32) + down_recv[3].astype(F32)
    new_table, new_state = adagrad(second_ref[...], sstate_ref[...], total)
    second_new[...] = new_table
    sstate_new[...] = new_state

    for k in range(1, NY):
        rows = rel_rows(c, lax.rem(y + k, NY), 0, 0, H_Y)
        back_copy(rows, ry_s.at[1, k], ry_r.at[1, k], dev_y(k)).wait_recv()
    c_rows = rel_rows(c, 0, 0, 0, H_CORE)
    last = back_copy(c_rows, co_s.at[1], co_r.at[1], dev_c)
    last.start()
    rows = rel_rows(1 - c, 0, 0, 0, H_CORE)
    back_copy(rows, co_s.at[1], co_r.at[1], dev_c).wait_recv()

    for way in (0, 1):
        for s in range(4):
            for q in gather_cuts(way, s):
                gather_copy(way, s, q).wait_send()
            for q in ring_cuts(way, s):
                ring_copy(way, s, q).wait_send()
    for k in range(1, NX):
        req_copy(k).wait_send()
        neg_copy(k).wait_send()
        dneg_copy(k).wait_send()
        rx_copy(k).wait_send()
        back_copy(x_rows, rx_s.at[1, k], rx_r.at[1, k], dev_x(k)).wait_send()
        for gi in range(3):
            serve_copy(k, gi).wait_send()
            c_copy(k, gi).wait_send()
    for k in range(1, NY):
        ry_copy(k).wait_send()
        back_copy(y_rows, ry_s.at[1, k], ry_r.at[1, k], dev_y(k)).wait_send()
    for k in range(1, NZ):
        rz_copy(k).wait_send()
        back_copy(mine_rows, rz_s.at[1, k], rz_r.at[1, k], dev_z(k)).wait_send()
    core_copy().wait_send()
    last.wait_send()


def step_call(*args):
    vmem = pl.BlockSpec(memory_space=pltpu.VMEM)
    dma = pltpu.SemaphoreType.DMA
    return pl.pallas_call(
        step_kernel,
        out_shape=(
            jax.ShapeDtypeStruct((D, R), F32),
            jax.ShapeDtypeStruct((1, R), F32),
            jax.ShapeDtypeStruct((D, R), F32),
            jax.ShapeDtypeStruct((1, R), F32),
            jax.ShapeDtypeStruct((2 * H_CORE, 128), BF16),
        ),
        in_specs=[vmem] * len(args),
        out_specs=(vmem,) * 5,
        scratch_shapes=[
            pltpu.VMEM((NZ, D, R), BF16),
            pltpu.VMEM((NX, 8, SLOTS), jnp.int32),
            pltpu.VMEM((NX, 8, SLOTS), jnp.int32),
            pltpu.VMEM((NX, 3, D, SLOTS), BF16),
            pltpu.VMEM((NX, 3, D, SLOTS), BF16),
            pltpu.VMEM((NX, D, 2 * NL), BF16),
            pltpu.VMEM((1, E), jnp.int32),
            pltpu.VMEM((3, D, K), BF16),
            pltpu.VMEM((D, E), F32),
            pltpu.VMEM((D, E), BF16),
            pltpu.VMEM((D, E), BF16),
            pltpu.VMEM((D, E), BF16),
            pltpu.VMEM((D, E), BF16),
            pltpu.VMEM((D, E), BF16),
            pltpu.VMEM((D, E), BF16),
            pltpu.VMEM((D, 2 * NL), BF16),
            pltpu.VMEM((NX, D, 2 * NL), BF16),
            pltpu.VMEM((NX, 3, D, SLOTS), BF16),
            pltpu.VMEM((NX, 3, D, SLOTS), BF16),
            pltpu.VMEM((4, D, R), BF16),
            pltpu.VMEM((4, D, R), BF16),
            pltpu.VMEM((4, D, R), BF16),
            pltpu.VMEM((4, D, R), BF16),
            pltpu.VMEM((2 * H_CORE, 128), BF16),
            pltpu.VMEM((H_CORE, 128), BF16),
            pltpu.VMEM((NY, H_Y, 128), BF16),
            pltpu.VMEM((NX, H_X, 128), BF16),
            pltpu.VMEM((NZ, H_Z, 128), BF16),
            pltpu.VMEM((H_Y, 128), BF16),
            pltpu.VMEM((H_X, 128), BF16),
            dma((2, 4, 4)), dma((2, 4, 4)),
            dma((NX,)), dma((NX,)),
            dma((NX, 3)), dma((NX, 3)),
            dma((NX,)), dma((NX,)),
            dma((NX, 3)), dma((NX, 3)),
            dma((NX,)), dma((NX,)),
            dma((2, 4, 4)), dma((2, 4, 4)),
            dma((2,)), dma((2,)),
            dma((2, NY)), dma((2, NY)),
            dma((2, NX)), dma((2, NX)),
            dma((2, NZ)), dma((2, NZ)),
        ],
        compiler_params=pltpu.CompilerParams(
            collective_id=0, has_side_effects=True, vmem_limit_bytes=60 * 1024 * 1024
        ),
        name="edge_step",
    )(*args)


def relation_kernel(grad_ref, diag_ref, state_ref, diag_new, state_new):
    i = pl.program_id(0)
    for j in range(2):
        tile = 2 * i + j
        start = pl.multiple_of((tile // 9) * H_CORE + (tile % 9) * D, 16)
        lanes = slice(j * 128, (j + 1) * 128)
        new, state = adagrad(diag_ref[:, lanes], state_ref[:, lanes], grad_ref[pl.ds(start, D)].astype(F32))
        diag_new[:, lanes] = new
        state_new[:, lanes] = state


def relation_call(grad, diag, state):
    lanes = lambda rows: pl.BlockSpec((rows, 256), lambda i: (0, i))
    return pl.pallas_call(
        relation_kernel,
        grid=(K // 256,),
        out_shape=(jax.ShapeDtypeStruct((D, K), F32), jax.ShapeDtypeStruct((1, K), F32)),
        in_specs=[pl.BlockSpec((2 * H_CORE, 128), lambda i: (0, 0)), lanes(D), lanes(1)],
        out_specs=(lanes(D), lanes(1)),
        compiler_params=pltpu.CompilerParams(vmem_limit_bytes=40 * 1024 * 1024),
        name="relation_update",
    )(grad, diag, state)


def on_device(
    first_table, first_state, second_table, second_state, relation_diag, relation_state,
    source_row, target_owner, target_row, relation_id, negative_id,
):
    diag = relation_diag.T
    negs = jnp.pad(negative_id[0], ((0, 0), (0, NL - NEG)), constant_values=-(1 << 20)).reshape(1, 2 * NL)
    first_new, first_state_new, second_new, second_state_new, rel_grad = step_call(
        first_table[0].T, first_state, second_table[0].T, second_state, diag,
        source_row, target_owner.reshape(1, E), target_row, relation_id, negs,
    )
    diag_new, state_new = relation_call(rel_grad, diag, relation_state.reshape(1, K))
    return (
        first_new.T[None], first_state_new, second_new.T[None], second_state_new,
        diag_new.T, state_new.reshape(K),
    )


def solution(mesh):
    in_specs = (
        P("group", "owner", None),
        P("group", "owner"),
        P("group", "owner", None),
        P("group", "owner"),
        P(),
        P(),
        P("group", "owner"),
        P("group", "owner", None),
        P("group", "owner"),
        P("group", "owner"),
        P("group", None, None),
    )
    out_specs = (
        P("group", "owner", None),
        P("group", "owner"),
        P("group", "owner", None),
        P("group", "owner"),
        P(),
        P(),
    )
    return jax.shard_map(
        on_device, mesh=mesh, in_specs=in_specs, out_specs=out_specs, check_vma=False
    )
```

time: 803 us -> 168 us (0.21)
  waiting for transfers between devices: 535 us -> 0 us
  Pallas kernels: 0 us -> 157 us
  blocking collectives: 78.5 us -> 0 us
  other arithmetic: 66.4 us -> 0.63 us
  local copies, waits for them, and re-layouts: 72.7 us -> 9.04 us
  starting transfers between devices: 26.2 us -> 0 us
  between operations: 14.2 us -> 0.67 us
  matrix products: 8.88 us -> 0 us
    unnamed x5 -> x0, waiting for transfers between devices: 269 us -> none
    psum x2 -> x0, waiting for transfers between devices: 253 us -> none  [the longest x1 130 us: bucket_grads(): lax.psum(d_negative.astype(jnp.bfloat16), 'owner').astype(jnp.float32)]
    pallas_call x0 -> x2, Pallas kernels: none -> 157 us  [the longest x1 152 us: step_call(): pl.pallas_call(step_kernel, out_shape=(jax.ShapeDtypeStruct((D, R), F32),...]
    unnamed x1 -> x0, blocking collectives: 78.5 us -> none
    scatter-add x4 -> x0, other arithmetic: 37.2 us -> none  [the longest x1 18.2 us: bucket_grads(): jax.ops.segment_sum(got_dst.reshape(parts * capacity, width).astype(jnp.f...]
    gather x7 -> x0, local copies, waits for them, and re-layouts: 27.2 us -> none  [the longest x1 8.19 us: bucket_grads(): served_dst = dst_copy[asked_dst]]
    all_to_all x3 -> x0, starting transfers between devices: 25.9 us -> none  [the longest x1 11.9 us: bucket_grads(): lax.all_to_all(dst_request, 'owner', split_axis=0, concat_axis=0, tiled=T...]
    unnamed x44 -> x12, local copies, waits for them, and re-layouts: 28.9 us -> 6.93 us
  transfers between devices with their start and end apart: 7 -> 0, of which waited for: 5 -> 0; matrix products, arithmetic and copies ran while one was open for 11% -> 0% of each run, Pallas kernels for 0% -> 0%
where the time goes in v1:
time: 168 us; the launch traced here: 167 us
  Pallas kernels  157 us (93%)
  local copies, waits for them, and re-layouts  9.04 us (5%)
    pallas_call x1, Pallas kernels, step_call(): pl.pallas_call(step_kernel, out_shape=(jax.ShapeDtypeStruct((D, R), F32),...  152 us
    unnamed x12, local copies, waits for them, and re-layouts  6.93 us
    pallas_call x1, Pallas kernels, relation_call(): pl.pallas_call(relation_kernel, grid=(K // 256,), out_shape=(jax.ShapeDty...  4.68 us

profile of v1, /device:TPU:1, one launch (start us, length us, event | category | flops | bytes accessed | tf_op | source)
XLA Modules:
  0.0 167.4 jit_solution(3117077437383743291)
XLA Ops:
  0.6 0.0 copy-start
  0.6 1.4 pad.4
  2.0 0.7 reshape.26.state_ref
  2.8 152.4 %edge_step.1 = (f32[400,512]{1,0:T(8,128)}, f32[1,512]{1,0:T(1,128)}, f32[400,512]{1,0:T(8,128)}, f32[1,512]{1,0:T(1,128)}, bf16[8192,128]{1,0:T(8,128)(2,1)}) custom-call(f32[400,512]{1,0:T(8,128)} %bitcast.19, f32[1,512]{1,0:T(1,128)} %fstate_ref.1, f32[400,512]{1,0:T(8,128)} %bitcast.20, f32[1,512]{1,0:T(1,128)} %sstate_ref.1, f32[400,2304]{1,0:T(8,128)} %bitcast.17, ...), custom_call_target="tpu_custom_call" | custom-call | tf_op jit(solution)/shard_map/edge_step/pallas_call | solution.py:488
  155.2 0.0 copy-done
  155.2 0.0 copy-start.1
  155.2 1.6 copy-done.1
  156.8 0.0 copy-start.3
  156.8 0.0 copy-start.2
  156.8 4.7 %relation_update.1 = (f32[400,2304]{1,0:T(8,128)}, f32[1,2304]{1,0:T(1,128)S(1)}) custom-call(bf16[8192,128]{1,0:T(8,128)(2,1)S(1)} %copy-done.1, f32[400,2304]{1,0:T(8,128)S(1)} %bitcast.18, f32[1,2304]{1,0:T(1,128)S(1)} %reshape.26.state_ref), custom_call_target="tpu_custom_call" | custom-call | tf_op jit(solution)/shard_map/relation_update/pallas_call | solution.py:562
  161.5 0.6 reduce
  162.1 2.1 %copy.21 = f32[1,512,400]{1,2,0:T(8,128)} copy(f32[1,512,400]{1,2,0:T(8,128)} %bitcast.22) | data formatting | bytes 1638400
  164.2 0.0 copy-done.3
  164.2 0.6 copy.22
  164.8 2.1 %copy.23 = f32[1,512,400]{1,2,0:T(8,128)} copy(f32[1,512,400]{1,2,0:T(8,128)} %bitcast.21) | data formatting | bytes 1638400
  166.8 0.0 copy-done.2
  166.9 0.6 copy.24
Async XLA Ops:
  0.6 154.6 %copy-start = (f32[2304,400]{0,1:T(8,128)S(1)}, f32[2304,400]{0,1:T(8,128)}, u32[]{:S(2)}) copy-start(f32[2304,400]{0,1:T(8,128)} %param.15) | copy-start | bytes 11059204
  155.2 1.6 copy-start.1
  156.8 7.4 %copy-start.3 = (f32[1,512]{1,0:T(1,128)S(1)}, f32[1,512]{1,0:T(1,128)}, u32[]{:S(2)}) copy-start(f32[1,512]{1,0:T(1,128)} %get-tuple-element.27) | copy-start | bytes 6148
  156.8 10.1 %copy-start.2 = (f32[1,512]{1,0:T(1,128)S(1)}, f32[1,512]{1,0:T(1,128)}, u32[]{:S(2)}) copy-start(f32[1,512]{1,0:T(1,128)} %get-tuple-element.29) | copy-start | bytes 6148

commit v2 on v1

v2 whole, which is shorter than its diff:
```python
import jax
import jax.numpy as jnp
from jax import lax
from jax.experimental import pallas as pl
from jax.experimental.pallas import tpu as pltpu
from jax.sharding import PartitionSpec as P

MESH = pl.DeviceIdType.MESH
F32 = jnp.float32
BF16 = jnp.bfloat16
LEARN = 0.1

D = 400
R = 512
E = 1024
BLOCK = 512
NEG = 100
NL = 128
K = 2304
NX, NY, NZ = 4, 4, 8
SLOTS = 256

GROUPS = ((7, 0, 1), (2, 6), (3, 4, 5))
SPOT = (1, 2, 3, 5, 6, 7, 4, 0)
CUTS = ((0, 96), (96, 112), (208, 96), (304, 96))
UP = (0, 7, 6, 5, 4)
DOWN = (0, 1, 2, 3, 4)
HALF = 208

H_CORE, H_PART, H_Y, H_X, H_Z = 4096, 2048, 512, 128, 16
Y_ROWS = (512, 400)
NEG_X, NEG_Z = 128, 16
NEG_ROWS = 512


def tile_rows(half, i):
    return half * H_CORE + (i * D if i < 5 else H_PART + (i - 5) * H_Y)


NN = (((1,), (0,)), ((), ()))
NT = (((1,), (1,)), ((), ()))
TN = (((0,), (0,)), ((), ()))


def dot(a, b, dims):
    return lax.dot_general(a, b, dims, preferred_element_type=F32)


def onehot(vec, base, n):
    rows = lax.broadcasted_iota(jnp.int32, (n, vec.shape[1]), 0)
    return jnp.where(rows == vec - base, 1.0, 0.0).astype(BF16)


def adagrad(table, state, grad):
    state_new = state + jnp.sum(grad * grad, axis=0, keepdims=True) * (1.0 / D)
    return table - LEARN * grad * (1.0 / jnp.sqrt(state_new)), state_new


def step_kernel(
    first_hbm, second_ref, diag_hbm, srow_ref, towner_ref, trow_ref, kind_ref, neg_ref,
    first_grad, second_grad, rel_out,
    first_ref, diag_ref, tabs, req, asked, serve, back, place_ref, neg_ids,
    splits, relrow, srcrow, query, dst, summand, dsource, dtarget, early,
    csend, crecv, up_send, up_recv, down_send, down_recv, lsum,
    neg_src, neg_xr, neg_xs, neg_zr, neg_out,
    relbuf, core_recv, y_recv, x_recv, z_recv, red_y, red_x,
    dg_s, ag_s, ag_r, rq_s, rq_r, sv_s, sv_r, cs_s, cs_r, rs_s, rs_r, nx_s, nx_r, nz_s, nz_r,
    co_s, co_r, ry_s, ry_r, rx_s, rx_r, rz_s, rz_r,
):
    g = lax.axis_index("group")
    o = lax.axis_index("owner")
    x, z = o // NZ, o % NZ
    y, c = g // 2, g % 2

    def dev_x(k):
        return (g, lax.rem(x + k, NX) * NZ + z)

    def dev_z(k):
        return (g, x * NZ + lax.rem(z + k, NZ))

    def dev_y(k):
        return (lax.rem(y + k, NY) * 2 + c, o)

    dev_c = (y * 2 + 1 - c, o)

    barrier = pltpu.get_barrier_semaphore()
    for peer in [dev_x(k) for k in range(1, NX)] + [dev_z(k) for k in range(1, NZ)] + [
        dev_y(k) for k in range(1, NY)
    ] + [dev_c]:
        pl.semaphore_signal(barrier, inc=1, device_id=peer, device_id_type=MESH)
    load_diag = pltpu.make_async_copy(diag_hbm, diag_ref, dg_s.at[0])
    load_first = pltpu.make_async_copy(first_hbm, first_ref, dg_s.at[1])
    load_first.start()
    load_diag.start()
    def table_lanes(offset):
        return pl.ds(SPOT[offset] * R, R)

    tabs[:, table_lanes(0)] = second_ref[...].astype(BF16)
    pl.semaphore_wait(barrier, NX + NZ + NY - 3 + 1)

    def remote(src, dst_, ss, rs, dev):
        return pltpu.make_async_remote_copy(
            src_ref=src, dst_ref=dst_, send_sem=ss, recv_sem=rs, device_id=dev, device_id_type=MESH
        )

    def gather_copy(way, step, q):
        path = UP if way == 0 else DOWN
        rows = pl.ds(*CUTS[q])
        return remote(
            tabs.at[rows, table_lanes(path[step])], tabs.at[rows, table_lanes(path[step + 1])],
            ag_s.at[way, step, q], ag_r.at[way, step, q], dev_z(1 if way == 0 else NZ - 1),
        )

    def gather_cuts(way, step):
        return range(4) if step < 3 else ((0, 1) if way == 0 else (2, 3))

    for q in range(4):
        for way in (0, 1):
            gather_copy(way, 0, q).start()

    def forward(step):
        for q in range(4):
            for way in (0, 1):
                if q in gather_cuts(way, step):
                    gather_copy(way, step, q).wait_recv()
                    if step < 3 and q in gather_cuts(way, step + 1):
                        gather_copy(way, step + 1, q).start()

    towner, trow = towner_ref[...], trow_ref[...]
    far = lax.rem(towner % NZ - z + NZ, NZ)
    side = lax.rem(towner // NZ - x + NX, NX)
    group = jnp.zeros_like(far)
    local = jnp.zeros_like(far)
    for gi, members in enumerate(GROUPS):
        for li, offset in enumerate(members):
            group = jnp.where(far == offset, gi, group)
            local = jnp.where(far == offset, li, local)
    kind_of = side * 8 + group
    mine = jnp.where(lax.broadcasted_iota(jnp.int32, (32, E), 0) == kind_of, 1.0, 0.0)
    before_mask = jnp.where(
        lax.broadcasted_iota(jnp.int32, (E, E), 0) < lax.broadcasted_iota(jnp.int32, (E, E), 1), 1.0, 0.0
    ).astype(BF16)
    before = dot(mine.astype(BF16), before_mask, NN)
    slot = jnp.sum(mine * before, axis=0, keepdims=True).astype(jnp.int32)
    for gi in range(3):
        place_ref[gi : gi + 1, :] = jnp.where(group == gi, side * SLOTS + slot, -1)
    value = local * R + trow + 1
    high = (value // 16).astype(F32)
    low = (value % 16).astype(F32)
    sends = jnp.concatenate([mine * high, mine * low], axis=0).astype(BF16)
    found = dot(sends, onehot(slot, 0, SLOTS), NT)
    wanted = (found[0:32] * 16.0 + found[32:64]).astype(jnp.int32) - 1
    asked[:, 0:SLOTS] = wanted[0:8]
    for k in range(1, NX):
        req[k] = wanted[8 * k : 8 * k + 8]

    def req_copy(k):
        return remote(req.at[k], asked.at[:, pl.ds((NX - k) * SLOTS, SLOTS)], rq_s.at[k], rq_r.at[NX - k], dev_x(k))

    for k in range(1, NX):
        req_copy(k).start()

    def neg_x_copy(u, k):
        rows = pl.ds(pl.multiple_of(lax.rem(x + k, NX) * NEG_X, NEG_X), NEG_X)
        return remote(neg_src.at[u, rows], neg_xr.at[u, NX - k], nx_s.at[u, 0, k], nx_r.at[u, 0, NX - k], dev_x(k))

    def neg_z_copy(u, k):
        rows = pl.ds(pl.multiple_of(lax.rem(z + k, NZ) * NEG_Z, NEG_Z), NEG_Z)
        return remote(neg_xs.at[u, rows], neg_zr.at[u, NZ - k], nz_s.at[u, 0, k], nz_r.at[u, 0, NZ - k], dev_z(k))

    def neg_zb_copy(u, k, way):
        at = lax.rem(z + k, NZ) if way else z
        rows = pl.ds(pl.multiple_of(x * NEG_X + at * NEG_Z, NEG_Z), NEG_Z)
        i = k if way else NZ - k
        return remote(neg_out.at[u, rows], neg_out.at[u, rows], nz_s.at[u, 1, k], nz_r.at[u, 1, i], dev_z(k))

    def neg_xb_copy(u, k, way):
        at = lax.rem(x + k, NX) if way else x
        rows = pl.ds(pl.multiple_of(at * NEG_X, NEG_X), NEG_X)
        i = k if way else NX - k
        return remote(neg_out.at[u, rows], neg_out.at[u, rows], nx_s.at[u, 1, k], nx_r.at[u, 1, i], dev_x(k))

    def neg_start(u):
        for k in range(1, NX):
            neg_x_copy(u, k).start()

    def neg_second(u):
        for k in range(1, NX):
            remote(neg_xr.at[u, k], neg_xr.at[u, k], nx_s.at[u, 0, k], nx_r.at[u, 0, k], dev_x(k)).wait_recv()
        total = neg_src[u, pl.ds(pl.multiple_of(x * NEG_X, NEG_X), NEG_X)].astype(F32)
        for k in range(1, NX):
            total = total + neg_xr[u, k].astype(F32)
        neg_xs[u] = total.astype(BF16)
        for k in range(1, NZ):
            neg_z_copy(u, k).start()

    def neg_third(u):
        for k in range(1, NZ):
            remote(neg_zr.at[u, k], neg_zr.at[u, k], nz_s.at[u, 0, k], nz_r.at[u, 0, k], dev_z(k)).wait_recv()
        total = neg_xs[u, pl.ds(pl.multiple_of(z * NEG_Z, NEG_Z), NEG_Z)].astype(F32)
        for k in range(1, NZ):
            total = total + neg_zr[u, k].astype(F32)
        neg_out[u, pl.ds(pl.multiple_of(x * NEG_X + z * NEG_Z, NEG_Z), NEG_Z)] = total.astype(BF16)
        for k in range(1, NZ):
            neg_zb_copy(u, k, 0).start()

    def neg_fourth(u):
        for k in range(1, NZ):
            neg_zb_copy(u, k, 1).wait_recv()
        for k in range(1, NX):
            neg_xb_copy(u, k, 0).start()

    def neg_last(u):
        for k in range(1, NX):
            neg_xb_copy(u, k, 1).wait_recv()

    neg_ids[...] = jnp.full((1, 2 * NL), -(1 << 20), jnp.int32)
    for b in range(2):
        neg_ids[:, b * NL : b * NL + NEG] = neg_ref[b : b + 1, :]
    negs = neg_ids[...] - o * R
    neg_src[0, 0:D] = dot(tabs[:, table_lanes(0)], onehot(negs, 0, R), NN).astype(BF16)
    for u in range(2):
        neg_src[u, D:NEG_ROWS] = jnp.zeros((NEG_ROWS - D, 2 * NL), BF16)
    neg_start(0)

    load_first.wait()
    first_copy = first_ref[...].astype(BF16)
    for b in range(2):
        lanes = slice(b * BLOCK, (b + 1) * BLOCK)
        srcrow[:, lanes] = dot(first_copy, onehot(srow_ref[:, lanes], 0, R), NN).astype(BF16)

    for k in range(1, NX):
        remote(req.at[k], asked.at[:, pl.ds(k * SLOTS, SLOTS)], rq_s.at[k], rq_r.at[k], dev_x(k)).wait_recv()

    def lanes_of(j):
        start = j * SLOTS
        return pl.ds(start if isinstance(j, int) else pl.multiple_of(start, SLOTS), SLOTS)

    def serve_copy(j, gi):
        return remote(
            serve.at[j, gi], back.at[gi, :, lanes_of(NX - j)], sv_s.at[j, gi], sv_r.at[NX - j, gi], dev_x(j)
        )

    def serve_rows(j, gi):
        members = GROUPS[gi]
        start = SPOT[members[0]] * R
        rows = len(members) * R
        want = asked[gi : gi + 1, lanes_of(j)]
        return dot(tabs[:, start : start + rows], onehot(want, 0, rows), NN).astype(BF16)

    def serve_group(gi):
        def body(j, carry):
            serve[j, gi] = serve_rows(j, gi)
            serve_copy(j, gi).start()
            return carry

        lax.fori_loop(1, NX, body, 0)

    def serve_own(gi):
        back[gi, :, 0:SLOTS] = serve_rows(0, gi)

    def relation_rows(n):
        def body(i, carry):
            lanes = pl.ds(pl.multiple_of(i * 256, 256), 256)
            pick = onehot(kind_ref[:, lanes], 0, K)
            relrow[:, lanes] = (
                dot(splits[0], pick, NN) + dot(splits[1], pick, NN) + dot(splits[2], pick, NN)
            )
            return carry

        lax.fori_loop(n, n + 1, body, 0)

    def wait_back(gi):
        for k in range(1, NX):
            remote(
                serve.at[k, gi], back.at[gi, :, lanes_of(k)], sv_s.at[k, gi], sv_r.at[k, gi], dev_x(k)
            ).wait_recv()

    def collect(gi, first):
        def body(b, carry):
            lanes = pl.ds(pl.multiple_of(b * 256, 256), 256)
            pick = onehot(place_ref[gi : gi + 1, lanes], 0, NX * SLOTS)
            rows = dot(back[gi], pick, NN).astype(BF16)
            dst[:, lanes] = rows if first else dst[:, lanes] + rows
            return carry

        lax.fori_loop(0, E // 256, body, 0)

    forward(0)
    serve_group(0)
    neg_second(0)
    serve_own(0)
    load_diag.wait()
    diag = diag_ref[...]
    high_part = diag.astype(BF16)
    rest = diag - high_part.astype(F32)
    splits[0] = high_part
    splits[1] = rest.astype(BF16)
    splits[2] = (rest - splits[1].astype(F32)).astype(BF16)
    forward(1)
    serve_group(1)
    neg_third(0)
    serve_own(1)
    relation_rows(0)
    forward(2)
    neg_fourth(0)
    relation_rows(1)
    forward(3)
    serve_group(2)
    serve_own(2)
    relation_rows(2)
    relation_rows(3)
    query[...] = (srcrow[...].astype(F32) * relrow[...]).astype(BF16)
    neg_last(0)

    scale = 1.0 / (BLOCK - 1 + NEG)
    for b in range(2):
        lanes = slice(b * BLOCK, (b + 1) * BLOCK)
        nl = slice(b * NL, (b + 1) * NL)
        q, n = query[:, lanes], neg_out[0, 0:D, nl]
        d_sampled = (scale * jax.nn.sigmoid(dot(q, n, TN))).astype(BF16)
        early[:, lanes] = dot(n, d_sampled, NT)
        neg_src[1, 0:D, nl] = dot(q, d_sampled, NN).astype(BF16)
    wait_back(0)
    collect(0, True)
    wait_back(1)
    collect(1, False)
    for half in range(2):
        at = half * H_CORE
        relbuf[at + 2000 : at + H_PART] = jnp.zeros((H_PART - 2000, 128), BF16)
        for i in range(4):
            gap = at + H_PART + i * H_Y + D
            relbuf[gap : gap + H_Y - D] = jnp.zeros((H_Y - D, 128), BF16)
    red_y[1, D:H_Y] = jnp.zeros((H_Y - D, 128), BF16)
    wait_back(2)
    collect(2, False)

    diagonal = lax.broadcasted_iota(jnp.int32, (BLOCK, BLOCK), 0) == lax.broadcasted_iota(
        jnp.int32, (BLOCK, BLOCK), 1
    )
    for b in range(2):
        lanes = slice(b * BLOCK, (b + 1) * BLOCK)
        q, t = query[:, lanes], dst[:, lanes]
        batch = dot(q, t, TN)
        d_batch = (
            jax.nn.sigmoid(jnp.where(diagonal, -batch, batch)) * jnp.where(diagonal, -1.0, scale)
        ).astype(BF16)
        d_query = dot(t, d_batch, NT) + early[:, lanes]
        dsource[:, lanes] = (d_query * relrow[:, lanes]).astype(BF16)
        summand[:, lanes] = (d_query * srcrow[:, lanes].astype(F32)).astype(BF16)
        dtarget[:, lanes] = dot(q, d_batch, NN).astype(BF16)

    def relation_pair(i):
        pick = onehot(kind_ref[...], i * 256, 256)
        pair = dot(summand[...], pick, NT).astype(BF16)
        for half in range(2):
            at = tile_rows(half, i)
            relbuf[at : at + D] = pair[:, half * 128 : half * 128 + 128]

    def rel_rows(cc, p, yy, xx, zz, n):
        at = cc * H_CORE + p * H_PART + yy * H_Y + xx * H_X + zz * H_Z
        return pl.ds(pl.multiple_of(at, 16), n)

    def core_copy(p):
        return remote(relbuf.at[rel_rows(1 - c, p, 0, 0, 0, H_PART)], core_recv.at[p], co_s.at[0, p], co_r.at[0, p], dev_c)

    def ry_copy(p, k):
        n = Y_ROWS[p]
        return remote(
            relbuf.at[rel_rows(c, p, lax.rem(y + k, NY), 0, 0, n)], y_recv.at[p, NY - k, pl.ds(0, n)],
            ry_s.at[0, p, k], ry_r.at[0, p, NY - k], dev_y(k),
        )

    def rx_copy(p, k):
        rows = pl.ds(pl.multiple_of(lax.rem(x + k, NX) * H_X, H_X), H_X)
        return remote(red_y.at[p, rows], x_recv.at[p, NX - k], rx_s.at[0, p, k], rx_r.at[0, p, NX - k], dev_x(k))

    def rz_copy(p, k):
        rows = pl.ds(pl.multiple_of(lax.rem(z + k, NZ) * H_Z, H_Z), H_Z)
        return remote(red_x.at[p, rows], z_recv.at[p, NZ - k], rz_s.at[0, p, k], rz_r.at[0, p, NZ - k], dev_z(k))

    def rzb_copy(p, k, way):
        rows = rel_rows(c, p, y, x, lax.rem(z + k, NZ) if way else z, H_Z)
        i = k if way else NZ - k
        return remote(rel_out.at[rows], rel_out.at[rows], rz_s.at[1, p, k], rz_r.at[1, p, i], dev_z(k))

    def rxb_copy(p, k, way):
        rows = rel_rows(c, p, y, lax.rem(x + k, NX) if way else x, 0, H_X)
        i = k if way else NX - k
        return remote(rel_out.at[rows], rel_out.at[rows], rx_s.at[1, p, k], rx_r.at[1, p, i], dev_x(k))

    def ryb_copy(p, k, way):
        rows = rel_rows(c, p, lax.rem(y + k, NY) if way else y, 0, 0, Y_ROWS[p])
        i = k if way else NY - k
        return remote(rel_out.at[rows], rel_out.at[rows], ry_s.at[1, p, k], ry_r.at[1, p, i], dev_y(k))

    def cb_copy(p, way):
        rows = rel_rows(1 - c if way else c, p, 0, 0, 0, H_PART)
        return remote(rel_out.at[rows], rel_out.at[rows], co_s.at[1, p], co_r.at[1, p], dev_c)

    def rel_y(p):
        remote(core_recv.at[p], core_recv.at[p], co_s.at[0, p], co_r.at[0, p], dev_c).wait_recv()
        own = rel_rows(c, p, 0, 0, 0, H_PART)
        relbuf[own] = (relbuf[own].astype(F32) + core_recv[p].astype(F32)).astype(BF16)
        for k in range(1, NY):
            ry_copy(p, k).start()

    def rel_x(p):
        n = Y_ROWS[p]
        for k in range(1, NY):
            part = y_recv.at[p, k, pl.ds(0, n)]
            remote(part, part, ry_s.at[0, p, k], ry_r.at[0, p, k], dev_y(k)).wait_recv()
        total = relbuf[rel_rows(c, p, y, 0, 0, n)].astype(F32)
        for k in range(1, NY):
            total = total + y_recv[p, k, 0:n].astype(F32)
        red_y[p, 0:n] = total.astype(BF16)
        for k in range(1, NX):
            rx_copy(p, k).start()

    def rel_z(p):
        for k in range(1, NX):
            remote(x_recv.at[p, k], x_recv.at[p, k], rx_s.at[0, p, k], rx_r.at[0, p, k], dev_x(k)).wait_recv()
        total = red_y[p, pl.ds(pl.multiple_of(x * H_X, H_X), H_X)].astype(F32)
        for k in range(1, NX):
            total = total + x_recv[p, k].astype(F32)
        red_x[p] = total.astype(BF16)
        for k in range(1, NZ):
            rz_copy(p, k).start()

    def rel_zb(p):
        for k in range(1, NZ):
            remote(z_recv.at[p, k], z_recv.at[p, k], rz_s.at[0, p, k], rz_r.at[0, p, k], dev_z(k)).wait_recv()
        total = red_x[p, pl.ds(pl.multiple_of(z * H_Z, H_Z), H_Z)].astype(F32)
        for k in range(1, NZ):
            total = total + z_recv[p, k].astype(F32)
        rel_out[rel_rows(c, p, y, x, z, H_Z)] = total.astype(BF16)
        for k in range(1, NZ):
            rzb_copy(p, k, 0).start()

    def rel_xb(p):
        for k in range(1, NZ):
            rzb_copy(p, k, 1).wait_recv()
        for k in range(1, NX):
            rxb_copy(p, k, 0).start()

    def rel_yb(p):
        for k in range(1, NX):
            rxb_copy(p, k, 1).wait_recv()
        for k in range(1, NY):
            ryb_copy(p, k, 0).start()

    def rel_cb(p):
        for k in range(1, NY):
            ryb_copy(p, k, 1).wait_recv()
        cb_copy(p, 0).start()

    def c_copy(j, gi):
        return remote(
            csend.at[j, gi], crecv.at[gi, :, lanes_of(NX - j)], cs_s.at[j, gi], cs_r.at[NX - j, gi], dev_x(j)
        )

    def spread(j, gi):
        pick = onehot(place_ref[gi : gi + 1, :], j * SLOTS, SLOTS)
        return dot(dtarget[...], pick, NT).astype(BF16)

    def send_group(gi):
        def body(j, carry):
            csend[j, gi] = spread(j, gi)
            c_copy(j, gi).start()
            return carry

        lax.fori_loop(1, NX, body, 0)

    def keep_group(gi):
        crecv[gi, :, 0:SLOTS] = spread(0, gi)

    def wait_c(gi):
        for k in range(1, NX):
            remote(
                csend.at[k, gi], crecv.at[gi, :, lanes_of(k)], cs_s.at[k, gi], cs_r.at[k, gi], dev_x(k)
            ).wait_recv()

    def line_sum(offset):
        gi = [offset in members for members in GROUPS].index(True)
        li = GROUPS[gi].index(offset)
        return dot(crecv[gi], onehot(asked[gi : gi + 1, :], li * R, R), NT)

    def ring_copy(way, s, q):
        send, recv = (up_send, up_recv) if way == 0 else (down_send, down_recv)
        rows = pl.ds(*CUTS[q])
        return remote(
            send.at[s, rows], recv.at[s, rows], rs_s.at[way, s, q], rs_r.at[way, s, q],
            dev_z(1 if way == 0 else NZ - 1),
        )

    def ring_cuts(way, s):
        return range(4) if s > 0 else ((0, 1) if way == 0 else (2, 3))

    def ring_part(s, turn):
        for i in range(2):
            for way in (0, 1):
                q = ((2, 3, 0, 1) if way == 0 else (0, 1, 2, 3))[2 * turn + i]
                if q not in ring_cuts(way, s):
                    continue
                send, recv = (up_send, up_recv) if way == 0 else (down_send, down_recv)
                at, size = CUTS[q]
                rows = slice(at, at + size)
                part = lsum[0 if s == 0 else way, rows]
                if s > 0 and q in ring_cuts(way, s - 1):
                    ring_copy(way, s - 1, q).wait_recv()
                    part = part + recv[s - 1, rows].astype(F32)
                send[s, rows] = part.astype(BF16)
                ring_copy(way, s, q).start()

    send_group(2)
    for i in range(5):
        relation_pair(i)
    core_copy(0).start()
    for i in range(5, 9):
        relation_pair(i)
    core_copy(1).start()
    rel_y(0)
    keep_group(2)
    rel_y(1)
    neg_start(1)
    first_grad[...] = dot(dsource[...], onehot(srow_ref[...], 0, R), NT)
    rel_x(0)
    wait_c(2)
    lsum[0] = line_sum(4)
    ring_part(0, 0)
    ring_part(0, 1)
    send_group(1)
    lsum[0] = line_sum(3)
    lsum[1] = line_sum(5)
    ring_part(1, 0)
    rel_z(0)
    rel_x(1)
    keep_group(1)
    ring_part(1, 1)
    neg_second(1)
    rel_zb(0)
    rel_z(1)
    send_group(0)
    wait_c(1)
    lsum[0] = line_sum(2)
    lsum[1] = line_sum(6)
    ring_part(2, 0)
    rel_xb(0)
    keep_group(0)
    rel_zb(1)
    ring_part(2, 1)
    neg_third(1)
    rel_yb(0)
    rel_xb(1)
    neg_fourth(1)
    wait_c(0)
    lsum[0] = line_sum(1)
    lsum[1] = line_sum(7)
    ring_part(3, 0)
    rel_yb(1)
    ring_part(3, 1)
    neg_last(1)
    total = line_sum(0) + dot(neg_out[1, 0:D], onehot(negs, 0, R), NT)
    rel_cb(0)

    for q in range(4):
        for way in (0, 1):
            ring_copy(way, 3, q).wait_recv()
    second_grad[...] = total + up_recv[3].astype(F32) + down_recv[3].astype(F32)
    rel_cb(1)
    cb_copy(0, 1).wait_recv()
    cb_copy(1, 1).wait_recv()

    for way in (0, 1):
        for s in range(4):
            for q in gather_cuts(way, s):
                gather_copy(way, s, q).wait_send()
            for q in ring_cuts(way, s):
                ring_copy(way, s, q).wait_send()
    for k in range(1, NX):
        req_copy(k).wait_send()
        for gi in range(3):
            serve_copy(k, gi).wait_send()
            c_copy(k, gi).wait_send()
    for u in range(2):
        for k in range(1, NX):
            neg_x_copy(u, k).wait_send()
            neg_xb_copy(u, k, 0).wait_send()
        for k in range(1, NZ):
            neg_z_copy(u, k).wait_send()
            neg_zb_copy(u, k, 0).wait_send()
    for p in range(2):
        core_copy(p).wait_send()
        cb_copy(p, 0).wait_send()
        for k in range(1, NY):
            ry_copy(p, k).wait_send()
            ryb_copy(p, k, 0).wait_send()
        for k in range(1, NX):
            rx_copy(p, k).wait_send()
            rxb_copy(p, k, 0).wait_send()
        for k in range(1, NZ):
            rz_copy(p, k).wait_send()
            rzb_copy(p, k, 0).wait_send()


def step_call(*args):
    vmem = pl.BlockSpec(memory_space=pltpu.VMEM)
    dma = pltpu.SemaphoreType.DMA
    return pl.pallas_call(
        step_kernel,
        out_shape=(
            jax.ShapeDtypeStruct((D, R), F32),
            jax.ShapeDtypeStruct((D, R), F32),
            jax.ShapeDtypeStruct((2 * H_CORE, 128), BF16),
        ),
        in_specs=[pl.BlockSpec(memory_space=pl.ANY) if i in (0, 2) else vmem for i in range(len(args))],
        out_specs=(vmem,) * 3,
        scratch_shapes=[
            pltpu.VMEM((D, R), F32),
            pltpu.VMEM((D, K), F32),
            pltpu.VMEM((D, NZ * R), BF16),
            pltpu.VMEM((NX, 8, SLOTS), jnp.int32),
            pltpu.VMEM((8, NX * SLOTS), jnp.int32),
            pltpu.VMEM((NX, 3, D, SLOTS), BF16),
            pltpu.VMEM((3, D, NX * SLOTS), BF16),
            pltpu.VMEM((8, E), jnp.int32),
            pltpu.VMEM((1, 2 * NL), jnp.int32),
            pltpu.VMEM((3, D, K), BF16),
            pltpu.VMEM((D, E), F32),
            pltpu.VMEM((D, E), BF16),
            pltpu.VMEM((D, E), BF16),
            pltpu.VMEM((D, E), BF16),
            pltpu.VMEM((D, E), BF16),
            pltpu.VMEM((D, E), BF16),
            pltpu.VMEM((D, E), BF16),
            pltpu.VMEM((D, E), F32),
            pltpu.VMEM((NX, 3, D, SLOTS), BF16),
            pltpu.VMEM((3, D, NX * SLOTS), BF16),
            pltpu.VMEM((4, D, R), BF16),
            pltpu.VMEM((4, D, R), BF16),
            pltpu.VMEM((4, D, R), BF16),
            pltpu.VMEM((4, D, R), BF16),
            pltpu.VMEM((2, D, R), F32),
            pltpu.VMEM((2, NEG_ROWS, 2 * NL), BF16),
            pltpu.VMEM((2, NX, NEG_X, 2 * NL), BF16),
            pltpu.VMEM((2, NEG_X, 2 * NL), BF16),
            pltpu.VMEM((2, NZ, NEG_Z, 2 * NL), BF16),
            pltpu.VMEM((2, NEG_ROWS, 2 * NL), BF16),
            pltpu.VMEM((2 * H_CORE, 128), BF16),
            pltpu.VMEM((2, H_PART, 128), BF16),
            pltpu.VMEM((2, NY, H_Y, 128), BF16),
            pltpu.VMEM((2, NX, H_X, 128), BF16),
            pltpu.VMEM((2, NZ, H_Z, 128), BF16),
            pltpu.VMEM((2, H_Y, 128), BF16),
            pltpu.VMEM((2, H_X, 128), BF16),
            dma((2,)),
            dma((2, 4, 4)), dma((2, 4, 4)),
            dma((NX,)), dma((NX,)),
            dma((NX, 3)), dma((NX, 3)),
            dma((NX, 3)), dma((NX, 3)),
            dma((2, 4, 4)), dma((2, 4, 4)),
            dma((2, 2, NX)), dma((2, 2, NX)),
            dma((2, 2, NZ)), dma((2, 2, NZ)),
            dma((2, 2)), dma((2, 2)),
            dma((2, 2, NY)), dma((2, 2, NY)),
            dma((2, 2, NX)), dma((2, 2, NX)),
            dma((2, 2, NZ)), dma((2, 2, NZ)),
        ],
        compiler_params=pltpu.CompilerParams(
            collective_id=0, has_side_effects=True, vmem_limit_bytes=60 * 1024 * 1024
        ),
        name="edge_step",
    )(*args)


def update_kernel(
    rel_grad, diag_ref, rstate_ref, first_ref, fstate_ref, first_grad, second_ref, sstate_ref, second_grad,
    diag_new, rstate_new, first_new, fstate_new, second_new, sstate_new,
):
    i = pl.program_id(0)
    for half in range(2):
        start = jnp.where(i < 5, i * D, H_PART + (i - 5) * H_Y) + half * H_CORE
        lanes = slice(half * 128, (half + 1) * 128)
        grad = rel_grad[pl.ds(pl.multiple_of(start, 16), D)].astype(F32)
        diag_new[:, lanes], rstate_new[:, lanes] = adagrad(diag_ref[:, lanes], rstate_ref[:, lanes], grad)

    @pl.when(i < 4)
    def _():
        first_new[...], fstate_new[...] = adagrad(first_ref[...], fstate_ref[...], first_grad[...])

    @pl.when(jnp.logical_and(i >= 4, i < 8))
    def _():
        second_new[...], sstate_new[...] = adagrad(second_ref[...], sstate_ref[...], second_grad[...])


def update_call(rel_grad, diag, rstate, first, fstate, first_grad, second, sstate, second_grad):
    pair = lambda rows: pl.BlockSpec((rows, 256), lambda i: (0, i))
    one = lambda rows: pl.BlockSpec((rows, 128), lambda i: (0, jnp.minimum(i, 3)))
    two = lambda rows: pl.BlockSpec((rows, 128), lambda i: (0, jnp.clip(i - 4, 0, 3)))
    shape = jax.ShapeDtypeStruct
    return pl.pallas_call(
        update_kernel,
        grid=(K // 256,),
        out_shape=(
            shape((D, K), F32), shape((1, K), F32), shape((D, R), F32), shape((1, R), F32),
            shape((D, R), F32), shape((1, R), F32),
        ),
        in_specs=[
            pl.BlockSpec((2 * H_CORE, 128), lambda i: (0, 0)),
            pair(D), pair(1), one(D), one(1), one(D), two(D), two(1), two(D),
        ],
        out_specs=(pair(D), pair(1), one(D), one(1), two(D), two(1)),
        compiler_params=pltpu.CompilerParams(vmem_limit_bytes=60 * 1024 * 1024),
        name="table_update",
    )(rel_grad, diag, rstate, first, fstate, first_grad, second, sstate, second_grad)


def on_device(
    first_table, first_state, second_table, second_state, relation_diag, relation_state,
    source_row, target_owner, target_row, relation_id, negative_id,
):
    diag, first, second = relation_diag.T, first_table[0].T, second_table[0].T
    first_grad, second_grad, rel_grad = step_call(
        first, second, diag,
        source_row, target_owner.reshape(1, E), target_row, relation_id, negative_id[0],
    )
    diag_new, state_new, first_new, first_state_new, second_new, second_state_new = update_call(
        rel_grad, diag, relation_state.reshape(1, K), first, first_state, first_grad, second, second_state, second_grad
    )
    return (
        first_new.T[None], first_state_new, second_new.T[None], second_state_new,
        diag_new.T, state_new.reshape(K),
    )


def solution(mesh):
    in_specs = (
        P("group", "owner", None),
        P("group", "owner"),
        P("group", "owner", None),
        P("group", "owner"),
        P(),
        P(),
        P("group", "owner"),
        P("group", "owner", None),
        P("group", "owner"),
        P("group", "owner"),
        P("group", None, None),
    )
    out_specs = (
        P("group", "owner", None),
        P("group", "owner"),
        P("group", "owner", None),
        P("group", "owner"),
        P(),
        P(),
    )
    return jax.shard_map(
        on_device, mesh=mesh, in_specs=in_specs, out_specs=out_specs, check_vma=False
    )
```

time: 168 us -> 140 us (0.83)
  Pallas kernels: 157 us -> 136 us
  local copies, waits for them, and re-layouts: 9.04 us -> 1.31 us
    pallas_call x1, Pallas kernels: 152 us -> 126 us  [step_call(): pl.pallas_call(step_kernel, out_shape=(jax.ShapeDtypeStruct((D, R), F32),...]
    unnamed x12 -> x0, local copies, waits for them, and re-layouts: 6.93 us -> none
    pallas_call x1, Pallas kernels: 4.68 us -> 9.97 us  [update_call(): pl.pallas_call(update_kernel, grid=(K // 256,), out_shape=(shape((D, K),...]
where the time goes in v2:
time: 140 us
  Pallas kernels  136 us (97%)
    pallas_call x1, Pallas kernels, step_call(): pl.pallas_call(step_kernel, out_shape=(jax.ShapeDtypeStruct((D, R), F32),...  126 us
    pallas_call x1, Pallas kernels, update_call(): pl.pallas_call(update_kernel, grid=(K // 256,), out_shape=(shape((D, K),...  9.97 us

profile of v2, /device:TPU:1, one launch (start us, length us, event | category | flops | bytes accessed | tf_op | source)
XLA Modules:
  0.0 139.6 jit_solution(14579800368061606823)
XLA Ops:
  0.6 1.3 reshape.22.rstate_ref
  1.9 126.4 %edge_step.1 = (f32[400,512]{1,0:T(8,128)}, f32[400,512]{1,0:T(8,128)}, bf16[8192,128]{1,0:T(8,128)(2,1)}) custom-call(f32[400,512]{1,0:T(8,128)} %bitcast.18, f32[400,512]{1,0:T(8,128)} %bitcast.20, f32[400,2304]{1,0:T(8,128)} %bitcast.16, s32[1,1024]{1,0:T(1,128)} %srow_ref.1, s32[1,1024]{1,0:T(1,128)} %bitcast.22, s32[1,1024]{1,0:T(1,128)} %trow_ref.1, ...), custom_call_target="tpu_custom_call" | custom-call | tf_op jit(solution)/shard_map/edge_step/pallas_call | solution.py:609
  128.3 10.0 %table_update.1 = (f32[400,2304]{1,0:T(8,128)}, f32[1,2304]{1,0:T(1,128)}, f32[400,512]{1,0:T(8,128)}, f32[1,512]{1,0:T(1,128)}, f32[400,512]{1,0:T(8,128)}, /*index=5*/f32[1,512]{1,0:T(1,128)}) custom-call(bf16[8192,128]{1,0:T(8,128)(2,1)} %get-tuple-element.15.rel_grad, f32[400,2304]{1,0:T(8,128)} %bitcast.17, f32[1,2304]{1,0:T(1,128)} %reshape.22.rstate_ref, ...), custom_call_target="tpu_custom_call" | custom-call | tf_op jit(solution)/shard_map/table_update/pallas_call | solution.py:701
  138.3 1.3 reduce

commit v3 on v2

--- a/solution.py
+++ b/solution.py
@@ -60,8 +60,8 @@
     first_hbm, second_ref, diag_hbm, srow_ref, towner_ref, trow_ref, kind_ref, neg_ref,
     first_grad, second_grad, rel_out,
     first_ref, diag_ref, tabs, req, asked, serve, back, place_ref, neg_ids,
-    splits, relrow, srcrow, query, dst, summand, dsource, dtarget, early,
-    csend, crecv, up_send, up_recv, down_send, down_recv, lsum,
+    splits, relrow, srcrow, query, query_t, dst, dsource, dtarget, early,
+    crecv, up_send, up_recv, down_send, down_recv, lsum,
     neg_src, neg_xr, neg_xs, neg_zr, neg_out,
     relbuf, core_recv, y_recv, x_recv, z_recv, red_y, red_x,
     dg_s, ag_s, ag_r, rq_s, rq_r, sv_s, sv_r, cs_s, cs_r, rs_s, rs_r, nx_s, nx_r, nz_s, nz_r,
@@ -321,6 +321,10 @@
         d_sampled = (scale * jax.nn.sigmoid(dot(q, n, TN))).astype(BF16)
         early[:, lanes] = dot(n, d_sampled, NT)
         neg_src[1, 0:D, nl] = dot(q, d_sampled, NN).astype(BF16)
+    neg_start(1)
+    for b in range(2):
+        lanes = slice(b * BLOCK, (b + 1) * BLOCK)
+        query_t[lanes, :] = query[:, lanes].astype(F32).T.astype(BF16)
     wait_back(0)
     collect(0, True)
     wait_back(1)
@@ -334,6 +338,7 @@
     red_y[1, D:H_Y] = jnp.zeros((H_Y - D, 128), BF16)
     wait_back(2)
     collect(2, False)
+    neg_second(1)
 
     diagonal = lax.broadcasted_iota(jnp.int32, (BLOCK, BLOCK), 0) == lax.broadcasted_iota(
         jnp.int32, (BLOCK, BLOCK), 1
@@ -341,18 +346,18 @@
     for b in range(2):
         lanes = slice(b * BLOCK, (b + 1) * BLOCK)
         q, t = query[:, lanes], dst[:, lanes]
-        batch = dot(q, t, TN)
+        batch = dot(query_t[lanes, :], t, NN)
         d_batch = (
             jax.nn.sigmoid(jnp.where(diagonal, -batch, batch)) * jnp.where(diagonal, -1.0, scale)
         ).astype(BF16)
         d_query = dot(t, d_batch, NT) + early[:, lanes]
         dsource[:, lanes] = (d_query * relrow[:, lanes]).astype(BF16)
-        summand[:, lanes] = (d_query * srcrow[:, lanes].astype(F32)).astype(BF16)
+        srcrow[:, lanes] = (d_query * srcrow[:, lanes].astype(F32)).astype(BF16)
         dtarget[:, lanes] = dot(q, d_batch, NN).astype(BF16)
 
     def relation_pair(i):
         pick = onehot(kind_ref[...], i * 256, 256)
-        pair = dot(summand[...], pick, NT).astype(BF16)
+        pair = dot(srcrow[...], pick, NT).astype(BF16)
         for half in range(2):
             at = tile_rows(half, i)
             relbuf[at : at + D] = pair[:, half * 128 : half * 128 + 128]
@@ -456,7 +461,7 @@
 
     def c_copy(j, gi):
         return remote(
-            csend.at[j, gi], crecv.at[gi, :, lanes_of(NX - j)], cs_s.at[j, gi], cs_r.at[NX - j, gi], dev_x(j)
+            serve.at[j, gi], crecv.at[gi, :, lanes_of(NX - j)], cs_s.at[j, gi], cs_r.at[NX - j, gi], dev_x(j)
         )
 
     def spread(j, gi):
@@ -465,7 +470,8 @@
 
     def send_group(gi):
         def body(j, carry):
-            csend[j, gi] = spread(j, gi)
+            serve_copy(j, gi).wait_send()
+            serve[j, gi] = spread(j, gi)
             c_copy(j, gi).start()
             return carry
 
@@ -477,7 +483,7 @@
     def wait_c(gi):
         for k in range(1, NX):
             remote(
-                csend.at[k, gi], crecv.at[gi, :, lanes_of(k)], cs_s.at[k, gi], cs_r.at[k, gi], dev_x(k)
+                serve.at[k, gi], crecv.at[gi, :, lanes_of(k)], cs_s.at[k, gi], cs_r.at[k, gi], dev_x(k)
             ).wait_recv()
 
     def line_sum(offset):
@@ -496,21 +502,20 @@
     def ring_cuts(way, s):
         return range(4) if s > 0 else ((0, 1) if way == 0 else (2, 3))
 
-    def ring_part(s, turn):
-        for i in range(2):
-            for way in (0, 1):
-                q = ((2, 3, 0, 1) if way == 0 else (0, 1, 2, 3))[2 * turn + i]
-                if q not in ring_cuts(way, s):
-                    continue
-                send, recv = (up_send, up_recv) if way == 0 else (down_send, down_recv)
-                at, size = CUTS[q]
-                rows = slice(at, at + size)
-                part = lsum[0 if s == 0 else way, rows]
-                if s > 0 and q in ring_cuts(way, s - 1):
-                    ring_copy(way, s - 1, q).wait_recv()
-                    part = part + recv[s - 1, rows].astype(F32)
-                send[s, rows] = part.astype(BF16)
-                ring_copy(way, s, q).start()
+    def ring_cut(s, i):
+        for way in (0, 1):
+            q = ((2, 3, 0, 1) if way == 0 else (0, 1, 2, 3))[i]
+            if q not in ring_cuts(way, s):
+                continue
+            send, recv = (up_send, up_recv) if way == 0 else (down_send, down_recv)
+            at, size = CUTS[q]
+            rows = slice(at, at + size)
+            part = lsum[0 if s == 0 else 2 * (s % 2) + way, rows]
+            if s > 0 and q in ring_cuts(way, s - 1):
+                ring_copy(way, s - 1, q).wait_recv()
+                part = part + recv[s - 1, rows].astype(F32)
+            send[s, rows] = part.astype(BF16)
+            ring_copy(way, s, q).start()
 
     send_group(2)
     for i in range(5):
@@ -522,51 +527,56 @@
     rel_y(0)
     keep_group(2)
     rel_y(1)
-    neg_start(1)
+    neg_third(1)
     first_grad[...] = dot(dsource[...], onehot(srow_ref[...], 0, R), NT)
     rel_x(0)
     wait_c(2)
     lsum[0] = line_sum(4)
-    ring_part(0, 0)
-    ring_part(0, 1)
-    send_group(1)
-    lsum[0] = line_sum(3)
-    lsum[1] = line_sum(5)
-    ring_part(1, 0)
+    ring_cut(0, 2)
+    ring_cut(0, 3)
+    ring_cut(0, 0)
+    ring_cut(0, 1)
+    lsum[2] = line_sum(3)
+    lsum[3] = line_sum(5)
     rel_z(0)
     rel_x(1)
+    send_group(1)
+    ring_cut(1, 0)
+    ring_cut(1, 1)
     keep_group(1)
-    ring_part(1, 1)
-    neg_second(1)
     rel_zb(0)
     rel_z(1)
+    ring_cut(1, 2)
+    ring_cut(1, 3)
+    rel_xb(0)
     send_group(0)
+    rel_zb(1)
     wait_c(1)
     lsum[0] = line_sum(2)
     lsum[1] = line_sum(6)
-    ring_part(2, 0)
-    rel_xb(0)
-    keep_group(0)
-    rel_zb(1)
-    ring_part(2, 1)
-    neg_third(1)
+    ring_cut(2, 0)
+    ring_cut(2, 1)
     rel_yb(0)
     rel_xb(1)
+    ring_cut(2, 2)
+    keep_group(0)
+    ring_cut(2, 3)
+    wait_c(0)
+    lsum[2] = line_sum(1)
+    lsum[3] = line_sum(7)
+    ring_cut(3, 0)
+    rel_yb(1)
+    ring_cut(3, 1)
     neg_fourth(1)
-    wait_c(0)
-    lsum[0] = line_sum(1)
-    lsum[1] = line_sum(7)
-    ring_part(3, 0)
-    rel_yb(1)
-    ring_part(3, 1)
+    rel_cb(0)
+    ring_cut(3, 2)
+    ring_cut(3, 3)
     neg_last(1)
-    total = line_sum(0) + dot(neg_out[1, 0:D], onehot(negs, 0, R), NT)
-    rel_cb(0)
-
+    lsum[0] = line_sum(0) + dot(neg_out[1, 0:D], onehot(negs, 0, R), NT)
     for q in range(4):
         for way in (0, 1):
             ring_copy(way, 3, q).wait_recv()
-    second_grad[...] = total + up_recv[3].astype(F32) + down_recv[3].astype(F32)
+    second_grad[...] = lsum[0] + up_recv[3].astype(F32) + down_recv[3].astype(F32)
     rel_cb(1)
     cb_copy(0, 1).wait_recv()
     cb_copy(1, 1).wait_recv()
@@ -580,7 +590,6 @@
     for k in range(1, NX):
         req_copy(k).wait_send()
         for gi in range(3):
-            serve_copy(k, gi).wait_send()
             c_copy(k, gi).wait_send()
     for u in range(2):
         for k in range(1, NX):
@@ -629,18 +638,17 @@
             pltpu.VMEM((D, E), F32),
             pltpu.VMEM((D, E), BF16),
             pltpu.VMEM((D, E), BF16),
-            pltpu.VMEM((D, E), BF16),
+            pltpu.VMEM((E, D), BF16),
             pltpu.VMEM((D, E), BF16),
             pltpu.VMEM((D, E), BF16),
             pltpu.VMEM((D, E), BF16),
             pltpu.VMEM((D, E), F32),
-            pltpu.VMEM((NX, 3, D, SLOTS), BF16),
             pltpu.VMEM((3, D, NX * SLOTS), BF16),
             pltpu.VMEM((4, D, R), BF16),
             pltpu.VMEM((4, D, R), BF16),
             pltpu.VMEM((4, D, R), BF16),
             pltpu.VMEM((4, D, R), BF16),
-            pltpu.VMEM((2, D, R), F32),
+            pltpu.VMEM((4, D, R), F32),
             pltpu.VMEM((2, NEG_ROWS, 2 * NL), BF16),
             pltpu.VMEM((2, NX, NEG_X, 2 * NL), BF16),
             pltpu.VMEM((2, NEG_X, 2 * NL), BF16),
@@ -667,50 +675,73 @@
             dma((2, 2, NZ)), dma((2, 2, NZ)),
         ],
         compiler_params=pltpu.CompilerParams(
-            collective_id=0, has_side_effects=True, vmem_limit_bytes=60 * 1024 * 1024
+            collective_id=0, has_side_effects=True, vmem_limit_bytes=56 * 1024 * 1024
         ),
         name="edge_step",
     )(*args)
 
 
+PARTS = 3
+
+
 def update_kernel(
-    rel_grad, diag_ref, rstate_ref, first_ref, fstate_ref, first_grad, second_ref, sstate_ref, second_grad,
-    diag_new, rstate_new, first_new, fstate_new, second_new, sstate_new,
+    rel_hbm, diag, rstate_ref, first, fstate_ref, fgrad_hbm, second, sstate_ref, sgrad_hbm,
+    diag_out, rstate_new, first_out, fstate_new, second_out, sstate_new,
+    rel_grad, fgrad, sgrad, diag_new, first_new, second_new, in_sem, out_sem,
 ):
-    i = pl.program_id(0)
-    for half in range(2):
-        start = jnp.where(i < 5, i * D, H_PART + (i - 5) * H_Y) + half * H_CORE
-        lanes = slice(half * 128, (half + 1) * 128)
-        grad = rel_grad[pl.ds(pl.multiple_of(start, 16), D)].astype(F32)
-        diag_new[:, lanes], rstate_new[:, lanes] = adagrad(diag_ref[:, lanes], rstate_ref[:, lanes], grad)
-
-    @pl.when(i < 4)
-    def _():
-        first_new[...], fstate_new[...] = adagrad(first_ref[...], fstate_ref[...], first_grad[...])
-
-    @pl.when(jnp.logical_and(i >= 4, i < 8))
-    def _():
-        second_new[...], sstate_new[...] = adagrad(second_ref[...], sstate_ref[...], second_grad[...])
+    def part(i):
+        return pl.ds(i * (K // PARTS), K // PARTS)
+
+    loads = [
+        pltpu.make_async_copy(src, dst, in_sem.at[i])
+        for i, (src, dst) in enumerate([(fgrad_hbm, fgrad), (sgrad_hbm, sgrad), (rel_hbm, rel_grad)])
+    ]
+    for load in loads:
+        load.start()
+    stores = [
+        pltpu.make_async_copy(src, dst, out_sem.at[i])
+        for i, (src, dst) in enumerate(
+            [(first_new, first_out), (second_new, second_out)]
+            + [(diag_new.at[:, part(i)], diag_out.at[:, part(i)]) for i in range(PARTS)]
+        )
+    ]
+    loads[0].wait()
+    first_new[...], fstate_new[...] = adagrad(first[...], fstate_ref[...], fgrad[...])
+    stores[0].start()
+    loads[1].wait()
+    second_new[...], sstate_new[...] = adagrad(second[...], sstate_ref[...], sgrad[...])
+    stores[1].start()
+    loads[2].wait()
+    for i in range(9):
+        for half in range(2):
+            at = tile_rows(half, i)
+            lanes = slice((2 * i + half) * 128, (2 * i + half + 1) * 128)
+            grad = rel_grad[at : at + D].astype(F32)
+            diag_new[:, lanes], state = adagrad(diag[:, lanes], rstate_ref[lanes].reshape(1, 128), grad)
+            rstate_new[lanes] = state.reshape(128)
+        if i % (9 // PARTS) == 9 // PARTS - 1:
+            stores[2 + i // (9 // PARTS)].start()
+    for store in stores:
+        store.wait()
 
 
 def update_call(rel_grad, diag, rstate, first, fstate, first_grad, second, sstate, second_grad):
-    pair = lambda rows: pl.BlockSpec((rows, 256), lambda i: (0, i))
-    one = lambda rows: pl.BlockSpec((rows, 128), lambda i: (0, jnp.minimum(i, 3)))
-    two = lambda rows: pl.BlockSpec((rows, 128), lambda i: (0, jnp.clip(i - 4, 0, 3)))
     shape = jax.ShapeDtypeStruct
+    vmem, hbm = pl.BlockSpec(memory_space=pltpu.VMEM), pl.BlockSpec(memory_space=pltpu.HBM)
+    table = pltpu.VMEM((D, R), F32)
     return pl.pallas_call(
         update_kernel,
-        grid=(K // 256,),
         out_shape=(
-            shape((D, K), F32), shape((1, K), F32), shape((D, R), F32), shape((1, R), F32),
+            shape((D, K), F32), shape((K,), F32), shape((D, R), F32), shape((1, R), F32),
             shape((D, R), F32), shape((1, R), F32),
         ),
-        in_specs=[
-            pl.BlockSpec((2 * H_CORE, 128), lambda i: (0, 0)),
-            pair(D), pair(1), one(D), one(1), one(D), two(D), two(1), two(D),
+        in_specs=[hbm, vmem, vmem, vmem, vmem, hbm, vmem, vmem, hbm],
+        out_specs=(hbm, vmem, hbm, vmem, hbm, vmem),
+        scratch_shapes=[
+            pltpu.VMEM((2 * H_CORE, 128), BF16), table, table, pltpu.VMEM((D, K), F32), table, table,
+            pltpu.SemaphoreType.DMA((3,)), pltpu.SemaphoreType.DMA((2 + PARTS,)),
         ],
-        out_specs=(pair(D), pair(1), one(D), one(1), two(D), two(1)),
-        compiler_params=pltpu.CompilerParams(vmem_limit_bytes=60 * 1024 * 1024),
+        compiler_params=pltpu.CompilerParams(vmem_limit_bytes=24 * 1024 * 1024),
         name="table_update",
     )(rel_grad, diag, rstate, first, fstate, first_grad, second, sstate, second_grad)
 
@@ -724,12 +755,15 @@
         first, second, diag,
         source_row, target_owner.reshape(1, E), target_row, relation_id, negative_id[0],
     )
+    first_grad, second_grad, rel_grad = (
+        pltpu.with_memory_space_constraint(v, pltpu.HBM) for v in (first_grad, second_grad, rel_grad)
+    )
     diag_new, state_new, first_new, first_state_new, second_new, second_state_new = update_call(
-        rel_grad, diag, relation_state.reshape(1, K), first, first_state, first_grad, second, second_state, second_grad
+        rel_grad, diag, relation_state, first, first_state, first_grad, second, second_state, second_grad
     )
     return (
         first_new.T[None], first_state_new, second_new.T[None], second_state_new,
-        diag_new.T, state_new.reshape(K),
+        diag_new.T, state_new,
     )
 
 

time: 140 us -> 129 us (0.921)
  Pallas kernels: 136 us -> 128 us
    pallas_call x1, Pallas kernels: 9.97 us -> 4.95 us  [update_call(): pl.pallas_call(update_kernel, out_shape=(shape((D, K), F32), shape((K,),...]
    pallas_call x1, Pallas kernels: 126 us -> 123 us  [step_call(): pl.pallas_call(step_kernel, out_shape=(jax.ShapeDtypeStruct((D, R), F32),...]
where the time goes in v3:
time: 129 us
  Pallas kernels  128 us (99%)
    pallas_call x1, Pallas kernels, step_call(): pl.pallas_call(step_kernel, out_shape=(jax.ShapeDtypeStruct((D, R), F32),...  123 us
    pallas_call x1, Pallas kernels, update_call(): pl.pallas_call(update_kernel, out_shape=(shape((D, K), F32), shape((K,),...  4.95 us

profile of v3, /device:TPU:1, one launch (start us, length us, event | category | flops | bytes accessed | tf_op | source)
XLA Modules:
  0.0 129.0 jit_solution(17394034983211754)
XLA Ops:
  0.6 0.0 copy-start.3
  0.6 0.0 copy-start
  0.7 0.0 copy-start.5
  0.7 0.0 copy-start.2
  0.7 0.0 copy-start.4
  0.7 0.0 copy-start.1
  0.7 123.1 %edge_step.1 = (f32[400,512]{1,0:T(8,128)}, f32[400,512]{1,0:T(8,128)}, bf16[8192,128]{1,0:T(8,128)(2,1)}) custom-call(f32[400,512]{1,0:T(8,128)} %bitcast.18, f32[400,512]{1,0:T(8,128)} %bitcast.20, f32[400,2304]{1,0:T(8,128)} %bitcast.16, s32[1,1024]{1,0:T(1,128)} %srow_ref.1, s32[1,1024]{1,0:T(1,128)} %bitcast.22, s32[1,1024]{1,0:T(1,128)} %trow_ref.1, ...), custom_call_target="tpu_custom_call" | custom-call | tf_op jit(solution)/shard_map/edge_step/pallas_call | solution.py:618
  123.8 0.0 copy-done.3
  123.8 0.0 copy-done
  123.8 0.0 copy-done.5
  123.8 0.0 copy-done.2
  123.9 0.0 copy-done.4
  123.9 0.0 copy-done.1
  123.9 4.9 %table_update.1 = (f32[400,2304]{1,0:T(8,128)}, f32[2304]{0:T(1024)}, f32[400,512]{1,0:T(8,128)}, f32[1,512]{1,0:T(1,128)}, f32[400,512]{1,0:T(8,128)}, /*index=5*/f32[1,512]{1,0:T(1,128)}) custom-call(bf16[8192,128]{1,0:T(8,128)(2,1)} %get-tuple-element.15.rel_hbm, f32[400,2304]{1,0:T(8,128)S(1)} %bitcast.17, f32[2304]{0:T(1024)S(1)} %copy-done.3, ...), custom_call_target="tpu_custom_call" | custom-call | tf_op jit(solution)/shard_map/table_update/pallas_call | solution.py:732
Async XLA Ops:
  0.6 123.2 %copy-start.3 = (f32[2304]{0:T(1024)S(1)}, f32[2304]{0:T(1024)}, u32[]{:S(2)}) copy-start(f32[2304]{0:T(1024)} %rstate_ref.1) | copy-start | bytes 27652
  0.6 123.2 %copy-start = (f32[2304,400]{0,1:T(8,128)S(1)}, f32[2304,400]{0,1:T(8,128)}, u32[]{:S(2)}) copy-start(f32[2304,400]{0,1:T(8,128)} %param.15) | copy-start | bytes 11059204
  0.7 123.2 %copy-start.5 = (f32[1,512]{1,0:T(1,128)S(1)}, f32[1,512]{1,0:T(1,128)}, u32[]{:S(2)}) copy-start(f32[1,512]{1,0:T(1,128)} %sstate_ref.1) | copy-start | bytes 6148
  0.7 123.2 %copy-start.2 = (f32[1,512,400]{1,2,0:T(8,128)S(1)}, f32[1,512,400]{1,2,0:T(8,128)}, u32[]{:S(2)}) copy-start(f32[1,512,400]{1,2,0:T(8,128)} %param.13) | copy-start | bytes 2457604
  0.7 123.2 %copy-start.4 = (f32[1,512]{1,0:T(1,128)S(1)}, f32[1,512]{1,0:T(1,128)}, u32[]{:S(2)}) copy-start(f32[1,512]{1,0:T(1,128)} %fstate_ref.1) | copy-start | bytes 6148
  0.7 123.2 %copy-start.1 = (f32[1,512,400]{1,2,0:T(8,128)S(1)}, f32[1,512,400]{1,2,0:T(8,128)}, u32[]{:S(2)}) copy-start(f32[1,512,400]{1,2,0:T(8,128)} %param.11) | copy-start | bytes 2457604

commit v4 on v3

--- a/solution.py
+++ b/solution.py
@@ -58,8 +58,8 @@
 
 def step_kernel(
     first_hbm, second_ref, diag_hbm, srow_ref, towner_ref, trow_ref, kind_ref, neg_ref,
-    first_grad, second_grad, rel_out,
-    first_ref, diag_ref, tabs, req, asked, serve, back, place_ref, neg_ids,
+    first_hbm_out, second_hbm_out, rel_hbm_out,
+    first_ref, diag_ref, first_grad, second_grad, rel_out, tabs, req, asked, serve, back, place_ref, neg_ids,
     splits, relrow, srcrow, query, query_t, dst, dsource, dtarget, early,
     crecv, up_send, up_recv, down_send, down_recv, lsum,
     neg_src, neg_xr, neg_xs, neg_zr, neg_out,
@@ -249,12 +249,13 @@
         return dot(tabs[:, start : start + rows], onehot(want, 0, rows), NN).astype(BF16)
 
     def serve_group(gi):
-        def body(j, carry):
+        def body(i, carry):
+            j = 2 - i + 3 * (i // 2)
             serve[j, gi] = serve_rows(j, gi)
             serve_copy(j, gi).start()
             return carry
 
-        lax.fori_loop(1, NX, body, 0)
+        lax.fori_loop(0, NX - 1, body, 0)
 
     def serve_own(gi):
         back[gi, :, 0:SLOTS] = serve_rows(0, gi)
@@ -302,8 +303,8 @@
     neg_third(0)
     serve_own(1)
     relation_rows(0)
+    neg_fourth(0)
     forward(2)
-    neg_fourth(0)
     relation_rows(1)
     forward(3)
     serve_group(2)
@@ -469,13 +470,14 @@
         return dot(dtarget[...], pick, NT).astype(BF16)
 
     def send_group(gi):
-        def body(j, carry):
+        def body(i, carry):
+            j = 2 - i + 3 * (i // 2)
             serve_copy(j, gi).wait_send()
             serve[j, gi] = spread(j, gi)
             c_copy(j, gi).start()
             return carry
 
-        lax.fori_loop(1, NX, body, 0)
+        lax.fori_loop(0, NX - 1, body, 0)
 
     def keep_group(gi):
         crecv[gi, :, 0:SLOTS] = spread(0, gi)
@@ -517,10 +519,10 @@
             send[s, rows] = part.astype(BF16)
             ring_copy(way, s, q).start()
 
-    send_group(2)
     for i in range(5):
         relation_pair(i)
     core_copy(0).start()
+    send_group(2)
     for i in range(5, 9):
         relation_pair(i)
     core_copy(1).start()
@@ -529,6 +531,8 @@
     rel_y(1)
     neg_third(1)
     first_grad[...] = dot(dsource[...], onehot(srow_ref[...], 0, R), NT)
+    keep_first = pltpu.make_async_copy(first_grad, first_hbm_out, dg_s.at[2])
+    keep_first.start()
     rel_x(0)
     wait_c(2)
     lsum[0] = line_sum(4)
@@ -577,9 +581,20 @@
         for way in (0, 1):
             ring_copy(way, 3, q).wait_recv()
     second_grad[...] = lsum[0] + up_recv[3].astype(F32) + down_recv[3].astype(F32)
+    keep_second = pltpu.make_async_copy(second_grad, second_hbm_out, dg_s.at[3])
+    keep_second.start()
+
+    def keep_rel(p, theirs):
+        rows = rel_rows(1 - c if theirs else c, p, 0, 0, 0, H_PART)
+        return pltpu.make_async_copy(rel_out.at[rows], rel_hbm_out.at[rows], dg_s.at[4 + 2 * p + theirs])
+
     rel_cb(1)
+    keep_rel(0, 0).start()
+    keep_rel(1, 0).start()
     cb_copy(0, 1).wait_recv()
+    keep_rel(0, 1).start()
     cb_copy(1, 1).wait_recv()
+    keep_rel(1, 1).start()
 
     for way in (0, 1):
         for s in range(4):
@@ -610,6 +625,11 @@
         for k in range(1, NZ):
             rz_copy(p, k).wait_send()
             rzb_copy(p, k, 0).wait_send()
+    keep_first.wait()
+    keep_second.wait()
+    for p in range(2):
+        keep_rel(p, 0).wait()
+        keep_rel(p, 1).wait()
 
 
 def step_call(*args):
@@ -623,10 +643,13 @@
             jax.ShapeDtypeStruct((2 * H_CORE, 128), BF16),
         ),
         in_specs=[pl.BlockSpec(memory_space=pl.ANY) if i in (0, 2) else vmem for i in range(len(args))],
-        out_specs=(vmem,) * 3,
+        out_specs=(pl.BlockSpec(memory_space=pl.ANY),) * 3,
         scratch_shapes=[
             pltpu.VMEM((D, R), F32),
             pltpu.VMEM((D, K), F32),
+            pltpu.VMEM((D, R), F32),
+            pltpu.VMEM((D, R), F32),
+            pltpu.VMEM((2 * H_CORE, 128), BF16),
             pltpu.VMEM((D, NZ * R), BF16),
             pltpu.VMEM((NX, 8, SLOTS), jnp.int32),
             pltpu.VMEM((8, NX * SLOTS), jnp.int32),
@@ -661,7 +684,7 @@
             pltpu.VMEM((2, NZ, H_Z, 128), BF16),
             pltpu.VMEM((2, H_Y, 128), BF16),
             pltpu.VMEM((2, H_X, 128), BF16),
-            dma((2,)),
+            dma((8,)),
             dma((2, 4, 4)), dma((2, 4, 4)),
             dma((NX,)), dma((NX,)),
             dma((NX, 3)), dma((NX, 3)),
@@ -681,7 +704,7 @@
     )(*args)
 
 
-PARTS = 3
+PARTS = 9
 
 
 def update_kernel(
@@ -694,7 +717,14 @@
 
     loads = [
         pltpu.make_async_copy(src, dst, in_sem.at[i])
-        for i, (src, dst) in enumerate([(fgrad_hbm, fgrad), (sgrad_hbm, sgrad), (rel_hbm, rel_grad)])
+        for i, (src, dst) in enumerate(
+            [
+                (rel_hbm.at[pl.ds(h * H_CORE + p * H_PART, H_PART)], rel_grad.at[pl.ds(h * H_CORE + p * H_PART, H_PART)])
+                for p in range(2)
+                for h in range(2)
+            ]
+            + [(fgrad_hbm, fgrad), (sgrad_hbm, sgrad)]
+        )
     ]
     for load in loads:
         load.start()
@@ -705,14 +735,10 @@
             + [(diag_new.at[:, part(i)], diag_out.at[:, part(i)]) for i in range(PARTS)]
         )
     ]
-    loads[0].wait()
-    first_new[...], fstate_new[...] = adagrad(first[...], fstate_ref[...], fgrad[...])
-    stores[0].start()
-    loads[1].wait()
-    second_new[...], sstate_new[...] = adagrad(second[...], sstate_ref[...], sgrad[...])
-    stores[1].start()
-    loads[2].wait()
     for i in range(9):
+        if i in (0, 5):
+            loads[2 * (i // 5)].wait()
+            loads[2 * (i // 5) + 1].wait()
         for half in range(2):
             at = tile_rows(half, i)
             lanes = slice((2 * i + half) * 128, (2 * i + half + 1) * 128)
@@ -721,6 +747,12 @@
             rstate_new[lanes] = state.reshape(128)
         if i % (9 // PARTS) == 9 // PARTS - 1:
             stores[2 + i // (9 // PARTS)].start()
+    loads[4].wait()
+    first_new[...], fstate_new[...] = adagrad(first[...], fstate_ref[...], fgrad[...])
+    stores[0].start()
+    loads[5].wait()
+    second_new[...], sstate_new[...] = adagrad(second[...], sstate_ref[...], sgrad[...])
+    stores[1].start()
     for store in stores:
         store.wait()
 
@@ -739,7 +771,7 @@
         out_specs=(hbm, vmem, hbm, vmem, hbm, vmem),
         scratch_shapes=[
             pltpu.VMEM((2 * H_CORE, 128), BF16), table, table, pltpu.VMEM((D, K), F32), table, table,
-            pltpu.SemaphoreType.DMA((3,)), pltpu.SemaphoreType.DMA((2 + PARTS,)),
+            pltpu.SemaphoreType.DMA((6,)), pltpu.SemaphoreType.DMA((2 + PARTS,)),
         ],
         compiler_params=pltpu.CompilerParams(vmem_limit_bytes=24 * 1024 * 1024),
         name="table_update",

time: 129 us -> 125 us (0.969)
  Pallas kernels: 128 us -> 124 us
    pallas_call x1, Pallas kernels: 123 us -> 119 us  [step_call(): pl.pallas_call(step_kernel, out_shape=(jax.ShapeDtypeStruct((D, R), F32),...]
where the time goes in v4:
time: 125 us; the launch traced here: 124 us
  Pallas kernels  124 us (99%)
    pallas_call x1, Pallas kernels, step_call(): pl.pallas_call(step_kernel, out_shape=(jax.ShapeDtypeStruct((D, R), F32),...  119 us
    pallas_call x1, Pallas kernels, update_call(): pl.pallas_call(update_kernel, out_shape=(shape((D, K), F32), shape((K,),...  4.49 us

profile of v4, /device:TPU:1, one launch (start us, length us, event | category | flops | bytes accessed | tf_op | source)
XLA Modules:
  0.0 124.5 jit_solution(9389258791212195053)
XLA Ops:
  0.6 0.0 copy-start.3
  0.6 0.0 copy-start
  0.7 0.0 copy-start.5
  0.7 0.0 copy-start.2
  0.7 0.0 copy-start.4
  0.7 0.0 copy-start.1
  0.7 119.0 %edge_step.1 = (f32[400,512]{1,0:T(8,128)}, f32[400,512]{1,0:T(8,128)}, bf16[8192,128]{1,0:T(8,128)(2,1)}) custom-call(f32[400,512]{1,0:T(8,128)} %bitcast.18, f32[400,512]{1,0:T(8,128)} %bitcast.20, f32[400,2304]{1,0:T(8,128)} %bitcast.16, s32[1,1024]{1,0:T(1,128)} %srow_ref.1, s32[1,1024]{1,0:T(1,128)} %bitcast.22, s32[1,1024]{1,0:T(1,128)} %trow_ref.1, ...), custom_call_target="tpu_custom_call" | custom-call | tf_op jit(solution)/shard_map/edge_step/pallas_call | solution.py:638
  119.7 0.0 copy-done.3
  119.7 0.0 copy-done
  119.8 0.0 copy-done.5
  119.8 0.0 copy-done.2
  119.8 0.0 copy-done.4
  119.8 0.0 copy-done.1
  119.8 4.5 %table_update.1 = (f32[400,2304]{1,0:T(8,128)}, f32[2304]{0:T(1024)}, f32[400,512]{1,0:T(8,128)}, f32[1,512]{1,0:T(1,128)}, f32[400,512]{1,0:T(8,128)}, /*index=5*/f32[1,512]{1,0:T(1,128)}) custom-call(bf16[8192,128]{1,0:T(8,128)(2,1)} %get-tuple-element.15.rel_hbm, f32[400,2304]{1,0:T(8,128)S(1)} %bitcast.17, f32[2304]{0:T(1024)S(1)} %copy-done.3, ...), custom_call_target="tpu_custom_call" | custom-call | tf_op jit(solution)/shard_map/table_update/pallas_call | solution.py:764
Async XLA Ops:
  0.6 119.1 %copy-start.3 = (f32[2304]{0:T(1024)S(1)}, f32[2304]{0:T(1024)}, u32[]{:S(2)}) copy-start(f32[2304]{0:T(1024)} %rstate_ref.1) | copy-start | bytes 27652
  0.6 119.1 %copy-start = (f32[2304,400]{0,1:T(8,128)S(1)}, f32[2304,400]{0,1:T(8,128)}, u32[]{:S(2)}) copy-start(f32[2304,400]{0,1:T(8,128)} %param.15) | copy-start | bytes 11059204
  0.7 119.1 %copy-start.5 = (f32[1,512]{1,0:T(1,128)S(1)}, f32[1,512]{1,0:T(1,128)}, u32[]{:S(2)}) copy-start(f32[1,512]{1,0:T(1,128)} %sstate_ref.1) | copy-start | bytes 6148
  0.7 119.1 %copy-start.2 = (f32[1,512,400]{1,2,0:T(8,128)S(1)}, f32[1,512,400]{1,2,0:T(8,128)}, u32[]{:S(2)}) copy-start(f32[1,512,400]{1,2,0:T(8,128)} %param.13) | copy-start | bytes 2457604
  0.7 119.1 %copy-start.4 = (f32[1,512]{1,0:T(1,128)S(1)}, f32[1,512]{1,0:T(1,128)}, u32[]{:S(2)}) copy-start(f32[1,512]{1,0:T(1,128)} %fstate_ref.1) | copy-start | bytes 6148
  0.7 119.1 %copy-start.1 = (f32[1,512,400]{1,2,0:T(8,128)S(1)}, f32[1,512,400]{1,2,0:T(8,128)}, u32[]{:S(2)}) copy-start(f32[1,512,400]{1,2,0:T(8,128)} %param.11) | copy-start | bytes 2457604
